TPU v7x, 256 devices: a whole 4x4x8 slice. The times are simulated.
256 devices in a mesh: shot: 8 (over y, core), rcv: 32 (over x, z).
Axes of the slice: x: 4, y: 4, z: 8, core: 2. Of those that a mesh axis runs over, the one named last changes fastest.
Arguments:
- blended: float32 [48, 512, 2048], P('shot', 'rcv'), may hold values from -60 to 60
- partners: int32 [48, 4], replicated, may hold values from -1 to 47, as said below
- offsets: int32 [48, 4], replicated, may hold values from -1024 to 1024
- fk_mask: int32 [2, 48, 1024], replicated, may hold values 0 or 1
Outputs:
- deblended: float32 [48, 512, 2048], P('shot', 'rcv')
- residual: float32 [48, 512, 2048], P('shot', 'rcv')
Inputs may be any that keep to these rules, and one draw needn't show every extreme that they name: `partners`: entries -1 mark empty slots and come after the filled ones; every other entry names a shot other than the row's own, at most 3 shots away, and no shot twice in a row; some shot has all 4 slots filled; the last shot is always named.
All inputs are finite; a program needn't handle non-finite values.
Results may differ from a plain program's by a relative error of at most 0.0003.
Values sent between devices are 32-bit elements; how exact they have to be, the bound alone decides.
A program may use at most 64 MiB of HBM per device.

v0:
```python
import math

import jax
import jax.numpy as jnp
import numpy as np
from jax import lax
from jax.experimental import pallas as pl
from jax.experimental.pallas import tpu as pltpu
from jax.sharding import PartitionSpec as P

ITERATIONS = 2
PARTNERS = 4
SHOTS = 48
SAMPLES = 2048
FREQS = 1024
ROWS = 16
GROUPS = 8
PITCH = 40
BASE = 16
TRACES = 2 * SHOTS

MESH = pl.DeviceIdType.MESH
BF16 = jnp.bfloat16
F32 = jnp.float32


def group_frequencies():
    j = np.arange(64)
    rows = [np.concatenate([16 * j, 8 + 16 * j])]
    for g in range(1, GROUPS):
        rows.append(np.concatenate([g + 16 * j, 16 - g + 16 * j]))
    return np.stack(rows)


def split_np(table):
    table = table.astype(np.float32)
    high = table.astype(jnp.bfloat16)
    low = (table - high.astype(np.float32)).astype(jnp.bfloat16)
    return high, low


def time_tables():
    kept = group_frequencies()
    n2 = np.arange(128)
    out = np.zeros((GROUPS, 256, 256))
    for g in range(GROUPS):
        phase = (n2[:, None] * kept[g][None, :]) % SAMPLES
        cos = np.cos(2 * np.pi * phase / SAMPLES)
        sin = np.sin(2 * np.pi * phase / SAMPLES)
        first = np.arange(128) < 64
        if g == 0:
            out[g, :128, :128] = np.where(first, cos, 0)
            out[g, :128, 128:] = np.where(first, -sin, 0)
            out[g, 128:, :128] = np.where(first, 0, cos)
            out[g, 128:, 128:] = np.where(first, 0, -sin)
        else:
            out[g, :128, :128] = cos
            out[g, :128, 128:] = -sin
            out[g, 128:, :128] = np.where(first, sin, -sin)
            out[g, 128:, 128:] = np.where(first, cos, -cos)
    return split_np(out)


def shot_tables():
    index = np.arange(SHOTS)
    phase = 2 * np.pi * ((index[:, None] * index[None, :]) % SHOTS) / SHOTS
    cos, sin = np.cos(phase), np.sin(phase)
    forward = np.block([[cos, sin], [-sin, cos]])
    inverse = np.block([[cos, -sin], [sin, cos]]) / (SHOTS * FREQS)
    return np.stack([forward, inverse])


def shot_operands():
    high, low = split_np(shot_tables())
    return np.concatenate([high, high], axis=2), low


def mask_order():
    order = group_frequencies().reshape(-1)
    out = np.zeros((FREQS, FREQS), np.float32)
    out[order, np.arange(FREQS)] = 1
    return out.astype(jnp.bfloat16)


C1, C2, C3 = (math.cos(math.pi * i / 8) for i in (1, 2, 3))


def radix16(x):
    a = [x[n] + x[n + 8] for n in range(8)]
    b = [x[n] - x[n + 8] for n in range(8)]
    e = [a[n] + a[n + 4] for n in range(4)]
    f = [a[n] - a[n + 4] for n in range(4)]
    p02, p13 = e[0] + e[2], e[1] + e[3]
    y0, y8 = p02 + p13, p02 - p13
    re4, im4 = e[0] - e[2], e[3] - e[1]
    m, q = C2 * (f[1] - f[3]), C2 * (f[1] + f[3])
    re2, re6 = f[0] + m, f[0] - m
    im2, im6 = -f[2] - q, f[2] - q
    c = [None] + [b[n] - b[8 - n] for n in (1, 2, 3)]
    d = [None] + [b[n] + b[8 - n] for n in (1, 2, 3)]
    up, down = b[0] + C2 * c[2], b[0] - C2 * c[2]
    v, w = C1 * c[1] + C3 * c[3], C3 * c[1] - C1 * c[3]
    re1, re7, re3, re5 = up + v, up - v, down + w, down - w
    p, t = C3 * d[1] + C1 * d[3], C2 * d[2] + b[4]
    q, u = C1 * d[1] - C3 * d[3], C2 * d[2] - b[4]
    im1, im7, im3, im5 = -p - t, t - p, -q - u, u - q
    return [(y0, y8), (re1, im1), (re2, im2), (re3, im3), (re4, im4), (re5, im5), (re6, im6), (re7, im7)]


def radix16_back(z):
    (w0, w8), (re1, im1), (re2, im2), (re3, im3), (re4, im4), (re5, im5), (re6, im6), (re7, im7) = z
    plus, minus = w0 + w8, w0 - w8
    ee = [plus + re4, minus - im4, plus - re4, minus + im4]
    m, q = C2 * (re2 - re6), C2 * (im2 + im6)
    eo = [re2 + re6, m - q, im6 - im2, -m - q]
    even = [ee[n] + eo[n] for n in range(4)] + [ee[n] - eo[n] for n in range(4)]
    s17, d17, s35, d35 = re1 + re7, re1 - re7, re3 + re5, re3 - re5
    t17, g17, t35, g35 = im1 + im7, im1 - im7, im3 + im5, im3 - im5
    pc = [None, C1 * d17 + C3 * d35, C2 * (s17 - s35), C3 * d17 - C1 * d35]
    ps = [None, C3 * t17 + C1 * t35, C2 * (g17 + g35), C1 * t17 - C3 * t35]
    odd = [None] * 8
    odd[0] = s17 + s35
    odd[4] = g35 - g17
    for n in (1, 2, 3):
        odd[n] = pc[n] - ps[n]
        odd[8 - n] = -pc[n] - ps[n]
    return [even[n] + odd[n] for n in range(8)] + [even[n] - odd[n] for n in range(8)]


def split(x):
    high = x.astype(BF16)
    return high, (x - high.astype(F32)).astype(BF16)


def dot(a, b):
    return lax.dot_general(a, b, (((1,), (0,)), ((), ())), preferred_element_type=F32)


def dot_t(a, b):
    return lax.dot_general(a, b, (((1,), (1,)), ((), ())), preferred_element_type=F32)


def fk_filter(sweep, res, out, kept, table_hi, table_lo, mix_hi, mix_lo, y_hi, y_lo, v, w, back):
    def forward_rows(block, _):
        recv, first = block // 3, (block % 3) * 256
        parts = []
        for half in range(2):
            x = [res[recv, pl.ds(first + half * 128 + n1, 8, stride=ROWS), :] for n1 in range(ROWS)]
            parts.append(radix16(x))
        row = pl.multiple_of(block * 16, 16)
        for g in range(GROUPS):
            for part in range(2):
                high, low = split(jnp.concatenate([parts[0][g][part], parts[1][g][part]], axis=0))
                y_hi[g, pl.ds(row, 16), part * 128:(part + 1) * 128] = high
                y_lo[g, pl.ds(row, 16), part * 128:(part + 1) * 128] = low
        return 0

    lax.fori_loop(0, TRACES // 16, forward_rows, 0)

    for g in range(GROUPS):
        z = dot(y_hi[g], table_hi[g]) + dot(y_lo[g], table_hi[g]) + dot(y_hi[g], table_lo[g])
        high, low = split(z)
        c = g * 256
        for source, at in ((high, 0), (low, 96)):
            v[at:at + 48, c:c + 128] = source[:48, :128]
            v[at:at + 48, c + 128:c + 256] = source[48:, :128]
            v[at + 48:at + 96, c:c + 128] = source[:48, 128:]
            v[at + 48:at + 96, c + 128:c + 256] = source[48:, 128:]

    for g in range(GROUPS):
        c = g * 256
        u = dot(mix_hi[0], v[:, c:c + 256]) + dot(mix_lo[0], v[:96, c:c + 256])
        keep = kept[sweep * SHOTS:(sweep + 1) * SHOTS, g * 128:(g + 1) * 128]
        keep = jnp.concatenate([keep, keep], axis=0)
        high, low = split(u * jnp.concatenate([keep, keep], axis=1))
        w[:96, c:c + 256] = high
        w[96:, c:c + 256] = low

    for g in range(GROUPS):
        c = g * 256
        z = dot(mix_hi[1], w[:, c:c + 256]) + dot(mix_lo[1], w[:96, c:c + 256])
        high, low = split(z)
        for source, at in ((high, y_hi), (low, y_lo)):
            at[g, :48, :128] = source[:48, :128]
            at[g, 48:, :128] = source[:48, 128:]
            at[g, :48, 128:] = source[48:, :128]
            at[g, 48:, 128:] = source[48:, 128:]

    for g in range(GROUPS):
        back[g] = (
            dot_t(y_hi[g], table_hi[g]) + dot_t(y_lo[g], table_hi[g]) + dot_t(y_hi[g], table_lo[g])
        )

    def inverse_rows(block, _):
        recv = block // 6
        shot = (block % 6) * 8
        row = pl.multiple_of(block * 8, 8)
        z = [
            (back[g, pl.ds(row, 8), 0:128], back[g, pl.ds(row, 8), 128:256])
            for g in range(GROUPS)
        ]
        x = radix16_back(z)
        for n1 in range(ROWS):
            out[recv, pl.ds(shot * PITCH + BASE + n1, 8, stride=PITCH), :] = x[n1]
        return 0

    lax.fori_loop(0, TRACES // 8, inverse_rows, 0)


def blend(partners, offsets, q, res, image):
    lane = lax.broadcasted_iota(jnp.int32, (ROWS, 128), 1)

    def one_shot(shot, sums):
        num, den = sums
        where = []
        for j in range(PARTNERS):
            partner, delay = partners[shot, j], offsets[shot, j]
            trace = jnp.where(partner >= 0, partner, SHOTS)
            rest = delay & 127
            where.append((trace * PITCH + BASE - (delay >> 7), rest, lane < 128 - rest))
        for recv in range(2):
            own = pl.multiple_of(shot * PITCH + BASE, 8)
            g = q[recv, pl.ds(own, ROWS), :]
            for start, rest, near in where:
                here = q[recv, pl.ds(start, ROWS), :]
                before = q[recv, pl.ds(start - 1, ROWS), :]
                g = g + pltpu.roll(jnp.where(near, here, before), rest, 1)
            at = pl.ds(pl.multiple_of(shot * ROWS, ROWS), ROWS)
            image[recv, at, :] = g
            num = num + res[recv, at, :] * g
            den = den + g * g
        return num, den

    zero = jnp.zeros((ROWS, 128), F32)
    return lax.fori_loop(0, SHOTS, one_shot, (zero, zero), unroll=2)


def kernel(
    groups, planes, columns,
    partners, offsets, blended, fk_mask, table_hi_h, table_lo_h, order_h, mix_hi, mix_lo,
    out_d, out_r,
    staged, res, q1, q2, image, send_d, send_r, y_hi, y_lo, v, w, back,
    table_hi, table_lo, order, kept, sums_mine, sums_got,
    load_sem, in_send, in_recv, out_send, out_recv, own_sem, sum_send, sum_recv,
):
    me = lax.axis_index("shot")
    place = lax.axis_index("rcv")
    plane, column = place // columns, place % columns

    loads = [
        pltpu.make_async_copy(table_hi_h, table_hi, load_sem.at[0]),
        pltpu.make_async_copy(table_lo_h, table_lo, load_sem.at[1]),
        pltpu.make_async_copy(order_h, order, load_sem.at[2]),
    ]
    for load in loads:
        load.start()

    shot_peers = [((lax.rem(me + k, groups), place)) for k in range(1, groups)]
    column_peers = [(me, plane * columns + lax.rem(column + k, columns)) for k in range(1, columns)]
    plane_peers = [(me, lax.rem(plane + k, planes) * columns + column) for k in range(1, planes)]
    peers = shot_peers + column_peers + plane_peers
    barrier = pltpu.get_barrier_semaphore()
    for peer in peers:
        pl.semaphore_signal(barrier, inc=1, device_id=peer, device_id_type=MESH)

    for shot in range(6):
        for half in range(2):
            for n1 in range(ROWS):
                at = half * 8 * 96 + shot * ROWS + n1
                staged[pl.ds(at, 8, stride=96), :] = blended[
                    shot, half * 8:(half + 1) * 8, n1 * 128:(n1 + 1) * 128
                ]

    pl.semaphore_wait(barrier, len(peers))

    mine = pl.ds(pl.multiple_of(me * 96, 8), 96)
    copies = []
    for k in range(1, groups):
        peer = shot_peers[k - 1]
        for recv in range(2):
            copies.append(pltpu.make_async_remote_copy(
                src_ref=staged.at[pl.ds(pl.multiple_of(peer[0] * 192 + recv * 96, 8), 96)],
                dst_ref=res.at[recv, mine],
                send_sem=in_send.at[k - 1, recv],
                recv_sem=in_recv.at[k - 1, recv],
                device_id=peer, device_id_type=MESH,
            ))
            copies[-1].start()
    own = []
    for recv in range(2):
        own.append(pltpu.make_async_copy(
            staged.at[pl.ds(pl.multiple_of(me * 192 + recv * 96, 8), 96)],
            res.at[recv, mine], own_sem.at[recv],
        ))
        own[-1].start()

    q1[...] = jnp.zeros_like(q1)
    q2[...] = jnp.zeros_like(q2)
    for load in loads:
        load.wait()
    kept[...] = dot(fk_mask[...].astype(F32).astype(BF16), order[...])

    for copy in own:
        copy.wait()
    for copy in copies:
        copy.wait()

    def all_sum(sweep, num, den):
        mine_sum = jnp.concatenate([num[:8] + num[8:], den[:8] + den[8:]], axis=0)
        slot = 0
        for stage, stage_peers in enumerate((shot_peers, column_peers, plane_peers)):
            sums_mine[sweep, stage] = mine_sum
            moves = []
            for peer in stage_peers:
                moves.append(pltpu.make_async_remote_copy(
                    src_ref=sums_mine.at[sweep, stage], dst_ref=sums_got.at[sweep, slot],
                    send_sem=sum_send.at[sweep, slot], recv_sem=sum_recv.at[sweep, slot],
                    device_id=peer, device_id_type=MESH,
                ))
                moves[-1].start()
                slot += 1
            for i, move in enumerate(moves):
                move.wait()
                mine_sum = mine_sum + sums_got[sweep, slot - len(moves) + i]
        return jnp.sum(mine_sum[:8], keepdims=True) / jnp.sum(mine_sum[8:], keepdims=True)

    common = (kept, table_hi, table_lo, mix_hi, mix_lo, y_hi, y_lo, v, w, back)
    fk_filter(0, res, q1, *common)
    step1 = all_sum(0, *blend(partners, offsets, q1, res, image))
    res[...] = res[...] - step1 * image[...]
    fk_filter(1, res, q2, *common)
    step2 = all_sum(1, *blend(partners, offsets, q2, res, image))

    def finish(first_shot):
        for recv in range(2):
            for i in range(6):
                shot = first_shot + i
                data = pl.ds(pl.multiple_of(shot * PITCH + BASE, 8), ROWS)
                at = pl.ds(pl.multiple_of(shot * ROWS, ROWS), ROWS)
                send_d[recv, shot] = step1 * q1[recv, data, :] + step2 * q2[recv, data, :]
                send_r[recv, shot] = res[recv, at, :] - step2 * image[recv, at, :]

    copies = []
    for k in range(1, groups):
        peer = shot_peers[k - 1]
        finish(peer[0] * 6)
        for recv in range(2):
            for which, (source, target) in enumerate(((send_d, out_d), (send_r, out_r))):
                copies.append(pltpu.make_async_remote_copy(
                    src_ref=source.at[recv, pl.ds(peer[0] * 6, 6)],
                    dst_ref=target.at[:, pl.ds(pl.multiple_of((me * 2 + recv) * ROWS, ROWS), ROWS)],
                    send_sem=out_send.at[k - 1, recv, which],
                    recv_sem=out_recv.at[k - 1, recv, which],
                    device_id=peer, device_id_type=MESH,
                ))
                copies[-1].start()
    finish(me * 6)
    own = []
    for recv in range(2):
        for which, (source, target) in enumerate(((send_d, out_d), (send_r, out_r))):
            own.append(pltpu.make_async_copy(
                source.at[recv, pl.ds(me * 6, 6)],
                target.at[:, pl.ds(pl.multiple_of((me * 2 + recv) * ROWS, ROWS), ROWS)],
                own_sem.at[2 + recv * 2 + which],
            ))
            own[-1].start()
    for copy in own:
        copy.wait()
    for copy in copies:
        copy.wait()


def natural(d_rows, r_rows, d_out, r_out):
    for source, target in ((d_rows, d_out), (r_rows, r_out)):
        for half in range(2):
            for n1 in range(ROWS):
                target[0, half * 8:(half + 1) * 8, n1 * 128:(n1 + 1) * 128] = source[
                    0, pl.ds(half * 128 + n1, 8, stride=ROWS), :
                ]


def solution(mesh):
    groups = mesh.shape["shot"]
    columns = 8 if mesh.shape["rcv"] % 8 == 0 else mesh.shape["rcv"]
    planes = mesh.shape["rcv"] // columns
    slots = groups - 1 + columns - 1 + planes - 1
    table_hi, table_lo = time_tables()
    mix_hi, mix_lo = shot_operands()
    order = mask_order()

    def body(blended, partners, offsets, fk_mask):
        vmem = pl.BlockSpec(memory_space=pltpu.VMEM)
        smem = pl.BlockSpec(memory_space=pltpu.SMEM)
        hbm = pl.BlockSpec(memory_space=pl.ANY)
        rows = jax.ShapeDtypeStruct((6, 16 * ROWS, 128), F32)
        d_rows, r_rows = pl.pallas_call(
            lambda *refs: kernel(groups, planes, columns, *refs),
            out_shape=(rows, rows),
            in_specs=[smem, smem, vmem, vmem, hbm, hbm, hbm, vmem, vmem],
            out_specs=(hbm, hbm),
            scratch_shapes=[
                pltpu.VMEM((16 * 96, 128), F32),
                pltpu.VMEM((2, SHOTS * ROWS, 128), F32),
                pltpu.VMEM((2, (SHOTS + 1) * PITCH, 128), F32),
                pltpu.VMEM((2, (SHOTS + 1) * PITCH, 128), F32),
                pltpu.VMEM((2, SHOTS * ROWS, 128), F32),
                pltpu.VMEM((2, SHOTS, ROWS, 128), F32),
                pltpu.VMEM((2, SHOTS, ROWS, 128), F32),
                pltpu.VMEM((GROUPS, TRACES, 256), BF16),
                pltpu.VMEM((GROUPS, TRACES, 256), BF16),
                pltpu.VMEM((192, 2 * FREQS), BF16),
                pltpu.VMEM((192, 2 * FREQS), BF16),
                pltpu.VMEM((GROUPS, TRACES, 256), F32),
                pltpu.VMEM((GROUPS, 256, 256), BF16),
                pltpu.VMEM((GROUPS, 256, 256), BF16),
                pltpu.VMEM((FREQS, FREQS), BF16),
                pltpu.VMEM((ITERATIONS * SHOTS, FREQS), F32),
                pltpu.VMEM((ITERATIONS, 3, 16, 128), F32),
                pltpu.VMEM((ITERATIONS, slots, 16, 128), F32),
                pltpu.SemaphoreType.DMA((3,)),
                pltpu.SemaphoreType.DMA((groups - 1, 2)),
                pltpu.SemaphoreType.DMA((groups - 1, 2)),
                pltpu.SemaphoreType.DMA((groups - 1, 2, 2)),
                pltpu.SemaphoreType.DMA((groups - 1, 2, 2)),
                pltpu.SemaphoreType.DMA((6,)),
                pltpu.SemaphoreType.DMA((ITERATIONS, slots)),
                pltpu.SemaphoreType.DMA((ITERATIONS, slots)),
            ],
            compiler_params=pltpu.CompilerParams(
                collective_id=0, has_side_effects=True, vmem_limit_bytes=48 * 2**20
            ),
            name="deblend",
        )(
            partners, offsets, blended, fk_mask.reshape(ITERATIONS * SHOTS, FREQS),
            jnp.asarray(table_hi), jnp.asarray(table_lo), jnp.asarray(order),
            jnp.asarray(mix_hi), jnp.asarray(mix_lo),
        )
        out = jax.ShapeDtypeStruct(blended.shape, F32)
        row_spec = pl.BlockSpec((1, 16 * ROWS, 128), lambda i: (i, 0, 0))
        out_spec = pl.BlockSpec((1, 16, SAMPLES), lambda i: (i, 0, 0))
        return pl.pallas_call(
            natural,
            grid=(6,),
            out_shape=(out, out),
            in_specs=[row_spec, row_spec],
            out_specs=(out_spec, out_spec),
            name="natural_order",
        )(d_rows, r_rows)

    in_specs = (P("shot", "rcv", None), P(), P(), P())
    out_specs = (P("shot", "rcv", None), P("shot", "rcv", None))
    return jax.shard_map(body, mesh=mesh, in_specs=in_specs, out_specs=out_specs, check_vma=False)
```

profile of v0, /device:TPU:1, one launch (start us, length us, event | category | flops | bytes accessed | tf_op | source)
XLA Modules:
  0.0 90.7 jit_solution(2332074589888045174)
XLA Ops:
  0.6 0.8 copy.11.refs_0_
  1.4 0.8 copy.12.refs_1_
  2.2 0.0 copy-start
  2.2 1.2 %copy-done = bf16[8,256,256]{2,1,0:T(8,128)(2,1)S(1)} copy-done((bf16[8,256,256]{2,1,0:T(8,128)(2,1)S(1)}, bf16[8,256,256]{2,1,0:T(8,128)(2,1)}, u32[]{:S(2)}) %copy-start) | copy-done | bytes 1048600
  3.4 0.0 copy-start.1
  3.4 1.2 %copy-done.1 = bf16[8,256,256]{2,1,0:T(8,128)(2,1)S(1)} copy-done((bf16[8,256,256]{2,1,0:T(8,128)(2,1)S(1)}, bf16[8,256,256]{2,1,0:T(8,128)(2,1)}, u32[]{:S(2)}) %copy-start.1) | copy-done | bytes 1048600
  4.6 0.0 copy-start.4
  4.6 1.1 %copy-done.4 = f32[6,16,2048]{2,1,0:T(8,128)S(1)} copy-done((f32[6,16,2048]{2,1,0:T(8,128)S(1)}, f32[6,16,2048]{2,1,0:T(8,128)}, u32[]{:S(2)}) %copy-start.4) | copy-done | bytes 786456
  5.7 0.0 copy-start.5
  5.7 1.0 %copy-done.5 = s32[2,48,1024]{2,1,0:T(8,128)S(1)} copy-done((s32[2,48,1024]{2,1,0:T(8,128)S(1)}, s32[2,48,1024]{2,1,0:T(8,128)}, u32[]{:S(2)}) %copy-start.5) | copy-done | bytes 393240
  6.7 0.0 copy-start.6
  6.7 0.9 copy-done.6
  7.6 0.0 copy-start.7
  7.6 0.8 copy-done.7
  8.4 75.7 %deblend.1 = (f32[6,256,128]{2,1,0:T(8,128)S(1)}, f32[6,256,128]{2,1,0:T(8,128)S(1)}) custom-call(s32[48,4]{1,0:T(8,128)S(1)} %copy.11.refs_0_, s32[48,4]{1,0:T(8,128)S(1)} %copy.12.refs_1_, f32[6,16,2048]{2,1,0:T(8,128)S(1)} %copy-done.4, s32[96,1024]{1,0:T(8,128)S(1)} %bitcast.1, bf16[8,256,256]{2,1,0:T(8,128)(2,1)S(1)} %copy-done.1, ...), custom_call_target="tpu_custom_call" | custom-call | tf_op jit(solution)/shard_map/deblend/pallas_call | solution.py:396
  84.2 0.0 copy-start.2
  84.2 0.9 copy-done.2
  85.1 0.0 copy-start.3
  85.1 0.9 copy-done.3
  86.0 4.8 %natural_order.1 = (f32[6,16,2048]{2,1,0:T(8,128)}, f32[6,16,2048]{2,1,0:T(8,128)}) custom-call(f32[6,256,128]{2,1,0:T(8,128)} %copy-done.2, f32[6,256,128]{2,1,0:T(8,128)} %copy-done.3), custom_call_target="tpu_custom_call" | custom-call | tf_op jit(solution)/shard_map/natural_order/pallas_call | solution.py:441
Async XLA Ops:
  2.2 1.2 %copy-start = (bf16[8,256,256]{2,1,0:T(8,128)(2,1)S(1)}, bf16[8,256,256]{2,1,0:T(8,128)(2,1)}, u32[]{:S(2)}) copy-start(bf16[8,256,256]{2,1,0:T(8,128)(2,1)} %constant.11.clone.refs_5_) | copy-start | bytes 3145732
  3.4 1.2 %copy-start.1 = (bf16[8,256,256]{2,1,0:T(8,128)(2,1)S(1)}, bf16[8,256,256]{2,1,0:T(8,128)(2,1)}, u32[]{:S(2)}) copy-start(bf16[8,256,256]{2,1,0:T(8,128)(2,1)} %constant.10.clone.refs_4_) | copy-start | bytes 3145732
  4.6 1.1 %copy-start.4 = (f32[6,16,2048]{2,1,0:T(8,128)S(1)}, f32[6,16,2048]{2,1,0:T(8,128)}, u32[]{:S(2)}) copy-start(f32[6,16,2048]{2,1,0:T(8,128)} %refs_2_.1) | copy-start | bytes 2359300
  5.7 1.0 %copy-start.5 = (s32[2,48,1024]{2,1,0:T(8,128)S(1)}, s32[2,48,1024]{2,1,0:T(8,128)}, u32[]{:S(2)}) copy-start(s32[2,48,1024]{2,1,0:T(8,128)} %param.12) | copy-start | bytes 1179652
  6.7 0.9 copy-start.6
  7.6 0.8 copy-start.7
  84.2 0.9 copy-start.2
  85.1 0.9 copy-start.3
where the time goes:
time: 91.2 us; the launch traced here: 90.7 us
  Pallas kernels  80.5 us (88%)
  local copies, waits for them, and re-layouts  9.58 us (11%)
    pallas_call x1, Pallas kernels, body(): pl.pallas_call(lambda *refs: kernel(groups, planes, columns, *refs), out_...  75.7 us
    unnamed x18, local copies, waits for them, and re-layouts  9.58 us
    pallas_call x1, Pallas kernels, body(): pl.pallas_call(natural, grid=(6,), out_shape=(out, out), in_specs=[row_sp...  4.78 us

commit v1 on v0

v1 whole, which is shorter than its diff:
```python
import math

import jax
import jax.numpy as jnp
import numpy as np
from jax import lax
from jax.experimental import pallas as pl
from jax.experimental.pallas import tpu as pltpu
from jax.sharding import PartitionSpec as P

ITERATIONS = 2
PARTNERS = 4
SHOTS = 48
SAMPLES = 2048
FREQS = 1024
ROWS = 16
GROUPS = 8
PITCH = 40
BASE = 16
TRACES = 2 * SHOTS

MESH = pl.DeviceIdType.MESH
BF16 = jnp.bfloat16
F32 = jnp.float32


def group_frequencies():
    j = np.arange(64)
    rows = [np.concatenate([16 * j, 8 + 16 * j])]
    for g in range(1, GROUPS):
        rows.append(np.concatenate([g + 16 * j, 16 - g + 16 * j]))
    return np.stack(rows)


def split_np(table):
    table = table.astype(np.float32)
    high = table.astype(jnp.bfloat16)
    low = (table - high.astype(np.float32)).astype(jnp.bfloat16)
    return high, low


def time_tables():
    kept = group_frequencies()
    n2 = np.arange(128)
    out = np.zeros((GROUPS, 256, 256))
    for g in range(GROUPS):
        phase = (n2[:, None] * kept[g][None, :]) % SAMPLES
        cos = np.cos(2 * np.pi * phase / SAMPLES)
        sin = np.sin(2 * np.pi * phase / SAMPLES)
        first = np.arange(128) < 64
        if g == 0:
            out[g, :128, :128] = np.where(first, cos, 0)
            out[g, :128, 128:] = np.where(first, -sin, 0)
            out[g, 128:, :128] = np.where(first, 0, cos)
            out[g, 128:, 128:] = np.where(first, 0, -sin)
        else:
            out[g, :128, :128] = cos
            out[g, :128, 128:] = -sin
            out[g, 128:, :128] = np.where(first, sin, -sin)
            out[g, 128:, 128:] = np.where(first, cos, -cos)
    return split_np(out)


def shot_tables():
    index = np.arange(SHOTS)
    phase = 2 * np.pi * ((index[:, None] * index[None, :]) % SHOTS) / SHOTS
    cos, sin = np.cos(phase), np.sin(phase)
    forward = np.block([[cos, sin], [-sin, cos]])
    inverse = np.block([[cos, -sin], [sin, cos]]) / (SHOTS * FREQS)
    return np.stack([forward, inverse])


def shot_operands():
    high, low = split_np(shot_tables())
    return np.concatenate([high, high], axis=2), low


def mask_order():
    order = group_frequencies().reshape(-1)
    out = np.zeros((FREQS, FREQS), np.float32)
    out[order, np.arange(FREQS)] = 1
    return out.astype(jnp.bfloat16)


C1, C2, C3 = (math.cos(math.pi * i / 8) for i in (1, 2, 3))


def radix16(x):
    a = [x[n] + x[n + 8] for n in range(8)]
    b = [x[n] - x[n + 8] for n in range(8)]
    e = [a[n] + a[n + 4] for n in range(4)]
    f = [a[n] - a[n + 4] for n in range(4)]
    p02, p13 = e[0] + e[2], e[1] + e[3]
    y0, y8 = p02 + p13, p02 - p13
    re4, im4 = e[0] - e[2], e[3] - e[1]
    m, q = C2 * (f[1] - f[3]), C2 * (f[1] + f[3])
    re2, re6 = f[0] + m, f[0] - m
    im2, im6 = -f[2] - q, f[2] - q
    c = [None] + [b[n] - b[8 - n] for n in (1, 2, 3)]
    d = [None] + [b[n] + b[8 - n] for n in (1, 2, 3)]
    up, down = b[0] + C2 * c[2], b[0] - C2 * c[2]
    v, w = C1 * c[1] + C3 * c[3], C3 * c[1] - C1 * c[3]
    re1, re7, re3, re5 = up + v, up - v, down + w, down - w
    p, t = C3 * d[1] + C1 * d[3], C2 * d[2] + b[4]
    q, u = C1 * d[1] - C3 * d[3], C2 * d[2] - b[4]
    im1, im7, im3, im5 = -p - t, t - p, -q - u, u - q
    return [(y0, y8), (re1, im1), (re2, im2), (re3, im3), (re4, im4), (re5, im5), (re6, im6), (re7, im7)]


def radix16_back(z):
    (w0, w8), (re1, im1), (re2, im2), (re3, im3), (re4, im4), (re5, im5), (re6, im6), (re7, im7) = z
    plus, minus = w0 + w8, w0 - w8
    ee = [plus + re4, minus - im4, plus - re4, minus + im4]
    m, q = C2 * (re2 - re6), C2 * (im2 + im6)
    eo = [re2 + re6, m - q, im6 - im2, -m - q]
    even = [ee[n] + eo[n] for n in range(4)] + [ee[n] - eo[n] for n in range(4)]
    s17, d17, s35, d35 = re1 + re7, re1 - re7, re3 + re5, re3 - re5
    t17, g17, t35, g35 = im1 + im7, im1 - im7, im3 + im5, im3 - im5
    pc = [None, C1 * d17 + C3 * d35, C2 * (s17 - s35), C3 * d17 - C1 * d35]
    ps = [None, C3 * t17 + C1 * t35, C2 * (g17 + g35), C1 * t17 - C3 * t35]
    odd = [None] * 8
    odd[0] = s17 + s35
    odd[4] = g35 - g17
    for n in (1, 2, 3):
        odd[n] = pc[n] - ps[n]
        odd[8 - n] = -pc[n] - ps[n]
    return [even[n] + odd[n] for n in range(8)] + [even[n] - odd[n] for n in range(8)]


def split(x):
    high = x.astype(BF16)
    return high, (x - high.astype(F32)).astype(BF16)


def dot(a, b):
    return lax.dot_general(a, b, (((1,), (0,)), ((), ())), preferred_element_type=F32)


HALO = 3
SENT = 9 * ROWS
NEAR = 12
EARLY = 8


def forward(source, u, table_hi, table_lo, mix_hi, mix_lo, y_hi, y_lo, v):
    def forward_rows(block, _):
        recv, first = block // 3, (block % 3) * 256
        parts = []
        for half in range(2):
            x = [source[recv, pl.ds(first + half * 128 + n1, 8, stride=ROWS), :] for n1 in range(ROWS)]
            parts.append(radix16(x))
        row = pl.multiple_of(block * 16, 16)
        for g in range(GROUPS):
            for part in range(2):
                high, low = split(jnp.concatenate([parts[0][g][part], parts[1][g][part]], axis=0))
                y_hi[g, pl.ds(row, 16), part * 128:(part + 1) * 128] = high
                y_lo[g, pl.ds(row, 16), part * 128:(part + 1) * 128] = low
        return 0

    lax.fori_loop(0, TRACES // 16, forward_rows, 0)

    for g in range(GROUPS):
        z = dot(y_hi[g], table_hi[g]) + dot(y_lo[g], table_hi[g]) + dot(y_hi[g], table_lo[g])
        high, low = split(z)
        c = g * 256
        for source_rows, at in ((high, 0), (low, 96)):
            v[at:at + 48, c:c + 128] = source_rows[:48, :128]
            v[at:at + 48, c + 128:c + 256] = source_rows[48:, :128]
            v[at + 48:at + 96, c:c + 128] = source_rows[:48, 128:]
            v[at + 48:at + 96, c + 128:c + 256] = source_rows[48:, 128:]

    for g in range(GROUPS):
        c = g * 256
        u[g] = dot(mix_hi[0], v[:, c:c + 256]) + dot(mix_lo[0], v[:96, c:c + 256])


def inverse(spectrum, sweep, q, sent, kept, back_hi, back_lo, mix_hi, mix_lo, y_hi, y_lo, w, back):
    for g in range(GROUPS):
        c = g * 256
        keep = kept[sweep * SHOTS:(sweep + 1) * SHOTS, g * 128:(g + 1) * 128]
        keep = jnp.concatenate([keep, keep], axis=0)
        high, low = split(spectrum(g) * jnp.concatenate([keep, keep], axis=1))
        w[:96, c:c + 256] = high
        w[96:, c:c + 256] = low

    for g in range(GROUPS):
        c = g * 256
        z = dot(mix_hi[1], w[:, c:c + 256]) + dot(mix_lo[1], w[:96, c:c + 256])
        high, low = split(z)
        for source, at in ((high, y_hi), (low, y_lo)):
            at[g, :48, :128] = source[:48, :128]
            at[g, 48:, :128] = source[:48, 128:]
            at[g, :48, 128:] = source[48:, :128]
            at[g, 48:, 128:] = source[48:, 128:]

    for g in range(GROUPS):
        back[g] = dot(y_hi[g], back_hi[g]) + dot(y_lo[g], back_hi[g]) + dot(y_hi[g], back_lo[g])

    def inverse_rows(block, _):
        recv = block // 6
        shot = (block % 6) * 8
        row = pl.multiple_of(block * 8, 8)
        z = [
            (back[g, pl.ds(row, 8), 0:128], back[g, pl.ds(row, 8), 128:256])
            for g in range(GROUPS)
        ]
        x = radix16_back(z)
        for n1 in range(ROWS):
            q[recv, pl.ds(shot * PITCH + BASE + n1, 8, stride=PITCH), :] = x[n1]
            sent[recv, pl.ds((shot + HALO) * ROWS + n1, 8, stride=ROWS), :] = x[n1]
        return 0

    lax.fori_loop(0, TRACES // 8, inverse_rows, 0)


def shift_terms(lane, partners, offsets, shot, first, blank):
    terms = []
    for j in range(PARTNERS):
        partner, delay = partners[j, shot], offsets[j, shot]
        trace = jnp.where(partner >= 0, jnp.clip(partner - first, 0, blank - 1), blank)
        rest = delay & 127
        terms.append((trace * PITCH + BASE - (delay >> 7), rest, lane < 128 - rest))
    return terms


def shifted(q, recv, term):
    start, rest, near = term
    here = q[recv, pl.ds(start, ROWS), :]
    before = q[recv, pl.ds(start - 1, ROWS), :]
    return pltpu.roll(jnp.where(near, here, before), rest, 1)


def blend_sums(partners, offsets, q, residual, image):
    lane = lax.broadcasted_iota(jnp.int32, (ROWS, 128), 1)
    chunk = 8

    def shots(block, sums):
        num, den = sums
        terms = [
            shift_terms(lane, partners, offsets, block * chunk + i, 0, SHOTS) for i in range(chunk)
        ]
        for i in range(chunk):
            shot = block * chunk + i
            for recv in range(2):
                g = q[recv, pl.ds(pl.multiple_of(shot * PITCH + BASE, 8), ROWS), :]
                for term in terms[i]:
                    g = g + shifted(q, recv, term)
                at = pl.ds(pl.multiple_of(shot * ROWS, ROWS), ROWS)
                num = num + residual(recv, at) * g
                den = den + g * g
                if image is not None:
                    image[recv, at, :] = g
        return num, den

    zero = jnp.zeros((ROWS, 128), F32)
    num, den = lax.fori_loop(0, SHOTS // chunk, shots, (zero, zero))

    def fold(x):
        return x[:4] + x[4:8] + x[8:12] + x[12:]

    return jnp.concatenate([fold(num), fold(den)], axis=0)


def kernel(
    groups,
    partners, offsets, blended_h, fk_mask_h, order_h, tables_h, mix_hi, mix_lo,
    out_d, out_r,
    blended, fk_mask, staged, res, q, image, sent1, sent2, got1, got2, more1, more2, near_d, rows_r,
    y_hi, y_lo, v, w, back, u0, u1, tables, order, kept, sums_mine, sums_got,
    load_sem, in_send, in_recv, bulk_send, bulk_recv, more_send, more_recv, own_sem,
    sum_send, sum_recv,
):
    me = lax.axis_index("shot")
    place = lax.axis_index("rcv")
    places = lax.axis_size("rcv")
    core = lax.rem(me, 2)
    mate = (me + 1 - 2 * core, place)
    shot_peers = [(lax.rem(me + k, groups), place) for k in range(1, groups)]
    place_peers = [(me, lax.rem(place + k, places)) for k in range(1, places)]
    peers = shot_peers + place_peers

    first_load = pltpu.make_async_copy(blended_h, blended, load_sem.at[0])
    first_load.start()
    loads = [
        pltpu.make_async_copy(fk_mask_h, fk_mask, load_sem.at[1]),
        pltpu.make_async_copy(order_h, order, load_sem.at[2]),
        pltpu.make_async_copy(tables_h, tables, load_sem.at[3]),
    ]

    barrier = pltpu.get_barrier_semaphore()
    for peer in peers:
        pl.semaphore_signal(barrier, inc=1, device_id=peer, device_id_type=MESH)

    first_load.wait()
    for load in loads:
        load.start()
    for shot in range(6):
        for half in range(2):
            for n1 in range(ROWS):
                at = half * 8 * 96 + shot * ROWS + n1
                staged[pl.ds(at, 8, stride=96), :] = blended[
                    shot, half * 8:(half + 1) * 8, n1 * 128:(n1 + 1) * 128
                ]

    pl.semaphore_wait(barrier, len(peers))

    mine = pl.ds(pl.multiple_of(me * 96, 8), 96)
    copies = []
    for k in range(1, groups):
        peer = shot_peers[k - 1]
        for recv in range(2):
            copies.append(pltpu.make_async_remote_copy(
                src_ref=staged.at[pl.ds(pl.multiple_of(peer[0] * 192 + recv * 96, 8), 96)],
                dst_ref=res.at[recv, mine],
                send_sem=in_send.at[k - 1, recv],
                recv_sem=in_recv.at[k - 1, recv],
                device_id=peer, device_id_type=MESH,
            ))
            copies[-1].start()
    own = []
    for recv in range(2):
        own.append(pltpu.make_async_copy(
            staged.at[pl.ds(pl.multiple_of(me * 192 + recv * 96, 8), 96)],
            res.at[recv, mine], own_sem.at[recv],
        ))
        own[-1].start()

    q[...] = jnp.zeros_like(q)
    near_d[...] = jnp.zeros_like(near_d)
    for sent in (sent1, sent2):
        for recv in range(2):
            blank = jnp.zeros((HALO * ROWS, 128), F32)
            sent[recv, :HALO * ROWS, :] = blank
            sent[recv, (HALO + SHOTS) * ROWS:, :] = blank
    for load in loads:
        load.wait()
    kept[...] = dot(fk_mask[...].astype(F32).astype(BF16), order[...])

    for copy in own:
        copy.wait()
    for copy in copies:
        copy.wait()

    def bulk_copies(field, sent, got):
        moves = []
        for k in range(1, groups):
            peer = shot_peers[k - 1]
            for recv in range(2):
                start = (12 * (peer[0] // 2) + 9 * lax.rem(peer[0], 2)) * ROWS
                moves.append(pltpu.make_async_remote_copy(
                    src_ref=sent.at[recv, pl.ds(pl.multiple_of(start, 8), SENT)],
                    dst_ref=got.at[me * 2 + recv],
                    send_sem=bulk_send.at[field, k - 1, recv],
                    recv_sem=bulk_recv.at[field, k - 1, recv],
                    device_id=peer, device_id_type=MESH,
                ))
        return moves

    def own_copies(field, sent, got):
        moves = []
        for recv in range(2):
            start = (12 * (me // 2) + 9 * core) * ROWS
            moves.append(pltpu.make_async_copy(
                sent.at[recv, pl.ds(pl.multiple_of(start, 8), SENT)],
                got.at[me * 2 + recv], own_sem.at[2 + field * 2 + recv],
            ))
            moves[-1].start()
        return moves

    def sum_start(sweep, stage, value):
        sums_mine[sweep, stage] = value
        first = 0 if stage == 0 else len(place_peers)
        moves = []
        for i, peer in enumerate((place_peers, shot_peers)[stage]):
            moves.append(pltpu.make_async_remote_copy(
                src_ref=sums_mine.at[sweep, stage], dst_ref=sums_got.at[sweep, first + i],
                send_sem=sum_send.at[sweep, first + i], recv_sem=sum_recv.at[sweep, first + i],
                device_id=peer, device_id_type=MESH,
            ))
            moves[-1].start()
        return moves

    def sum_end(sweep, stage, value, moves):
        first = 0 if stage == 0 else len(place_peers)
        for i, move in enumerate(moves):
            move.wait_recv()
            value = value + sums_got[sweep, first + i]
        return value

    def ratio(value):
        return jnp.sum(value[:4], keepdims=True) / jnp.sum(value[4:], keepdims=True)

    def more_copy(field, got, more):
        at = pl.ds(pl.multiple_of(6 * (1 - core) * ROWS, 8), HALO * ROWS)
        move = pltpu.make_async_remote_copy(
            src_ref=got.at[:, at], dst_ref=more, send_sem=more_send.at[field],
            recv_sem=more_recv.at[field], device_id=mate, device_id_type=MESH,
        )
        move.start()
        return move

    ahead = (tables.at[0], tables.at[1], mix_hi, mix_lo, y_hi, y_lo, v)
    behind = (kept, tables.at[2], tables.at[3], mix_hi, mix_lo, y_hi, y_lo, w, back)

    forward(res, u0, *ahead)
    inverse(lambda g: u0[g], 0, q, sent1, *behind)
    bulk1 = bulk_copies(0, sent1, got1)
    for move in bulk1[:EARLY]:
        move.start()
    own1 = own_copies(0, sent1, got1)
    value = blend_sums(partners, offsets, q, lambda recv, at: res[recv, at, :], image)
    stage0 = sum_start(0, 0, value)
    forward(image, u1, *ahead)
    value = sum_end(0, 0, value, stage0)
    stage1 = sum_start(0, 1, value)
    for move in bulk1[EARLY:]:
        move.start()
    value = sum_end(0, 1, value, stage1)
    step1 = ratio(value)

    inverse(lambda g: u0[g] - step1 * u1[g], 1, q, sent2, *behind)
    bulk2 = bulk_copies(1, sent2, got2)
    for move in bulk2:
        move.start()
    own2 = own_copies(1, sent2, got2)
    value = blend_sums(
        partners, offsets, q, lambda recv, at: res[recv, at, :] - step1 * image[recv, at, :], None
    )
    stage2 = sum_start(1, 0, value)
    for move in own1:
        move.wait()
    for move in bulk1:
        move.wait()
    forward1 = more_copy(0, got1, more1)
    value = sum_end(1, 0, value, stage2)
    stage3 = sum_start(1, 1, value)
    for move in own2:
        move.wait()
    for move in bulk2:
        move.wait()
    forward2 = more_copy(1, got2, more2)
    value = sum_end(1, 1, value, stage3)
    step2 = ratio(value)

    def gather_direct(recv, _):
        for i in range(9):
            at = pl.ds(pl.multiple_of(recv * (NEAR + 1) * PITCH + (HALO * core + i) * PITCH + BASE, 8), ROWS)
            rows = slice(i * ROWS, (i + 1) * ROWS)
            near_d[0, at, :] = step1 * got1[recv, rows, :] + step2 * got2[recv, rows, :]
        return 0

    def gather_more(recv, _):
        for i in range(HALO):
            at = pl.ds(pl.multiple_of(recv * (NEAR + 1) * PITCH + (9 * (1 - core) + i) * PITCH + BASE, 8), ROWS)
            rows = slice(i * ROWS, (i + 1) * ROWS)
            near_d[0, at, :] = step1 * more1[recv, rows, :] + step2 * more2[recv, rows, :]
        return 0

    lax.fori_loop(0, 16, gather_direct, 0)
    forward1.wait()
    forward2.wait()
    lax.fori_loop(0, 16, gather_more, 0)

    lane = lax.broadcasted_iota(jnp.int32, (ROWS, 128), 1)
    first_shot = me * 6

    def finish(i, _):
        terms = shift_terms(lane, partners, offsets, first_shot + i, first_shot - HALO, NEAR)
        for recv in range(16):
            trace = recv * (NEAR + 1) * PITCH
            g = near_d[0, pl.ds(pl.multiple_of(trace + (HALO + i) * PITCH + BASE, 8), ROWS), :]
            for start, rest, near in terms:
                g = g + shifted(near_d, 0, (start + trace, rest, near))
            old = staged[pl.ds(pl.multiple_of(recv * 96 + i * ROWS, 8), ROWS), :]
            rows_r[recv * ROWS:(recv + 1) * ROWS, :] = old - g
        for half in range(2):
            for n1 in range(ROWS):
                at = (half * 8 * (NEAR + 1) + HALO + i) * PITCH + BASE + n1
                block = (i, slice(half * 8, (half + 1) * 8), slice(n1 * 128, (n1 + 1) * 128))
                out_d[block] = near_d[0, pl.ds(at, 8, stride=(NEAR + 1) * PITCH), :]
                out_r[block] = rows_r[pl.ds(half * 128 + n1, 8, stride=ROWS), :]
        return 0

    lax.fori_loop(0, 6, finish, 0)

    for move in stage0 + stage1 + stage2 + stage3:
        move.wait_send()


def solution(mesh):
    groups = mesh.shape["shot"]
    peers = groups - 1 + mesh.shape["rcv"] - 1
    table_hi, table_lo = time_tables()
    tables = np.stack([table_hi, table_lo, table_hi.swapaxes(1, 2), table_lo.swapaxes(1, 2)])
    mix_hi, mix_lo = shot_operands()
    order = mask_order()

    def body(blended, partners, offsets, fk_mask):
        vmem = pl.BlockSpec(memory_space=pltpu.VMEM)
        smem = pl.BlockSpec(memory_space=pltpu.SMEM)
        hbm = pl.BlockSpec(memory_space=pltpu.HBM)
        out = jax.ShapeDtypeStruct(blended.shape, F32)
        dma = pltpu.SemaphoreType.DMA
        return pl.pallas_call(
            lambda *refs: kernel(groups, *refs),
            out_shape=(out, out),
            in_specs=[smem, smem, hbm, hbm, hbm, hbm, vmem, vmem],
            out_specs=(vmem, vmem),
            scratch_shapes=[
                pltpu.VMEM(blended.shape, F32),
                pltpu.VMEM((ITERATIONS * SHOTS, FREQS), jnp.int32),
                pltpu.VMEM((16 * 96, 128), F32),
                pltpu.VMEM((2, SHOTS * ROWS, 128), F32),
                pltpu.VMEM((2, (SHOTS + 1) * PITCH, 128), F32),
                pltpu.VMEM((2, SHOTS * ROWS, 128), F32),
                pltpu.VMEM((2, (SHOTS + 2 * HALO) * ROWS, 128), F32),
                pltpu.VMEM((2, (SHOTS + 2 * HALO) * ROWS, 128), F32),
                pltpu.VMEM((16, SENT, 128), F32),
                pltpu.VMEM((16, SENT, 128), F32),
                pltpu.VMEM((16, HALO * ROWS, 128), F32),
                pltpu.VMEM((16, HALO * ROWS, 128), F32),
                pltpu.VMEM((1, 16 * (NEAR + 1) * PITCH, 128), F32),
                pltpu.VMEM((16 * ROWS, 128), F32),
                pltpu.VMEM((GROUPS, TRACES, 256), BF16),
                pltpu.VMEM((GROUPS, TRACES, 256), BF16),
                pltpu.VMEM((192, 2 * FREQS), BF16),
                pltpu.VMEM((192, 2 * FREQS), BF16),
                pltpu.VMEM((GROUPS, TRACES, 256), F32),
                pltpu.VMEM((GROUPS, TRACES, 256), F32),
                pltpu.VMEM((GROUPS, TRACES, 256), F32),
                pltpu.VMEM((4, GROUPS, 256, 256), BF16),
                pltpu.VMEM((FREQS, FREQS), BF16),
                pltpu.VMEM((ITERATIONS * SHOTS, FREQS), F32),
                pltpu.VMEM((ITERATIONS, 2, 8, 128), F32),
                pltpu.VMEM((ITERATIONS, peers, 8, 128), F32),
                dma((4,)),
                dma((groups - 1, 2)),
                dma((groups - 1, 2)),
                dma((ITERATIONS, groups - 1, 2)),
                dma((ITERATIONS, groups - 1, 2)),
                dma((ITERATIONS,)),
                dma((ITERATIONS,)),
                dma((6,)),
                dma((ITERATIONS, peers)),
                dma((ITERATIONS, peers)),
            ],
            compiler_params=pltpu.CompilerParams(
                collective_id=0, has_side_effects=True, vmem_limit_bytes=56 * 2**20
            ),
            name="deblend",
        )(
            partners.T, offsets.T, blended, fk_mask.reshape(ITERATIONS * SHOTS, FREQS),
            jnp.asarray(order), jnp.asarray(tables), jnp.asarray(mix_hi), jnp.asarray(mix_lo),
        )

    in_specs = (P("shot", "rcv", None), P(), P(), P())
    out_specs = (P("shot", "rcv", None), P("shot", "rcv", None))
    return jax.shard_map(body, mesh=mesh, in_specs=in_specs, out_specs=out_specs, check_vma=False)
```

time: 91.2 us -> 70.4 us (0.77)
  Pallas kernels: 80.5 us -> 65.4 us
  local copies, waits for them, and re-layouts: 9.58 us -> 4.13 us
    pallas_call x2 -> x1, Pallas kernels: 80.5 us -> 65.4 us  [body(): pl.pallas_call(lambda *refs: kernel(groups, *refs), out_shape=(out, out),...]
    unnamed x18 -> x2, local copies, waits for them, and re-layouts: 9.58 us -> 4.13 us
where the time goes in v1:
time: 70.4 us; the launch traced here: 70.1 us
  Pallas kernels  65.4 us (93%)
  local copies, waits for them, and re-layouts  4.13 us (6%)
    pallas_call x1, Pallas kernels, body(): pl.pallas_call(lambda *refs: kernel(groups, *refs), out_shape=(out, out),...  65.4 us
    unnamed x2, local copies, waits for them, and re-layouts  4.13 us

profile of v1, /device:TPU:1, one launch (start us, length us, event | category | flops | bytes accessed | tf_op | source)
XLA Modules:
  0.0 70.1 jit_solution(15053180259589908055)
XLA Ops:
  0.6 65.4 %deblend.1 = (f32[6,16,2048]{2,1,0:T(8,128)}, f32[6,16,2048]{2,1,0:T(8,128)}) custom-call(s32[4,48]{1,0:T(4,128)} %bitcast.4, s32[4,48]{1,0:T(4,128)} %bitcast.5, f32[6,16,2048]{2,1,0:T(8,128)} %refs_2_.1, s32[96,1024]{1,0:T(8,128)} %bitcast.3, bf16[1024,1024]{1,0:T(8,128)(2,1)} %constant.8.clone.refs_4_, bf16[4,8,256,256]{3,2,1,0:T(8,128)(2,1)} %constant.9.clone.refs_5_, ...), custom_call_target="tpu_custom_call" | custom-call | tf_op jit(solution)/shard_map/deblend/pallas_call | solution.py:504
  66.0 2.1 %copy.12 = f32[6,16,2048]{2,1,0:T(8,128)} copy(f32[6,16,2048]{2,1,0:T(8,128)} %get-tuple-element.4) | data formatting | bytes 1572864
  68.1 2.1 %copy.13 = f32[6,16,2048]{2,1,0:T(8,128)} copy(f32[6,16,2048]{2,1,0:T(8,128)} %get-tuple-element.5) | data formatting | bytes 1572864

commit v2 on v1

v2 whole, which is shorter than its diff:
```python
import math

import jax
import jax.numpy as jnp
import numpy as np
from jax import lax
from jax.experimental import pallas as pl
from jax.experimental.pallas import tpu as pltpu
from jax.sharding import PartitionSpec as P

ITERATIONS = 2
PARTNERS = 4
SHOTS = 48
SAMPLES = 2048
FREQS = 1024
ROWS = 16
GROUPS = 8
PITCH = 40
BASE = 16
TRACES = 2 * SHOTS

MESH = pl.DeviceIdType.MESH
BF16 = jnp.bfloat16
F32 = jnp.float32


def group_frequencies():
    j = np.arange(64)
    rows = [np.concatenate([16 * j, 8 + 16 * j])]
    for g in range(1, GROUPS):
        rows.append(np.concatenate([g + 16 * j, 16 - g + 16 * j]))
    return np.stack(rows)


def split_np(table):
    table = table.astype(np.float32)
    high = table.astype(jnp.bfloat16)
    low = (table - high.astype(np.float32)).astype(jnp.bfloat16)
    return high, low


def time_tables():
    kept = group_frequencies()
    n2 = np.arange(128)
    out = np.zeros((GROUPS, 256, 256))
    for g in range(GROUPS):
        phase = (n2[:, None] * kept[g][None, :]) % SAMPLES
        cos = np.cos(2 * np.pi * phase / SAMPLES)
        sin = np.sin(2 * np.pi * phase / SAMPLES)
        first = np.arange(128) < 64
        if g == 0:
            out[g, :128, :128] = np.where(first, cos, 0)
            out[g, :128, 128:] = np.where(first, -sin, 0)
            out[g, 128:, :128] = np.where(first, 0, cos)
            out[g, 128:, 128:] = np.where(first, 0, -sin)
        else:
            out[g, :128, :128] = cos
            out[g, :128, 128:] = -sin
            out[g, 128:, :128] = np.where(first, sin, -sin)
            out[g, 128:, 128:] = np.where(first, cos, -cos)
    return split_np(out)


def shot_tables():
    index = np.arange(SHOTS)
    phase = 2 * np.pi * ((index[:, None] * index[None, :]) % SHOTS) / SHOTS
    cos, sin = np.cos(phase), np.sin(phase)
    forward = np.block([[cos, sin], [-sin, cos]])
    inverse = np.block([[cos, -sin], [sin, cos]]) / (SHOTS * FREQS)
    return np.stack([forward, inverse])


def shot_operands():
    high, low = split_np(shot_tables())
    return np.concatenate([high, high], axis=2), low


def mask_order():
    order = group_frequencies().reshape(-1)
    out = np.zeros((FREQS, FREQS), np.float32)
    out[order, np.arange(FREQS)] = 1
    return out.astype(jnp.bfloat16)


C1, C2, C3 = (math.cos(math.pi * i / 8) for i in (1, 2, 3))


def radix16(x):
    a = [x[n] + x[n + 8] for n in range(8)]
    b = [x[n] - x[n + 8] for n in range(8)]
    e = [a[n] + a[n + 4] for n in range(4)]
    f = [a[n] - a[n + 4] for n in range(4)]
    p02, p13 = e[0] + e[2], e[1] + e[3]
    y0, y8 = p02 + p13, p02 - p13
    re4, im4 = e[0] - e[2], e[3] - e[1]
    m, q = C2 * (f[1] - f[3]), C2 * (f[1] + f[3])
    re2, re6 = f[0] + m, f[0] - m
    im2, im6 = -f[2] - q, f[2] - q
    c = [None] + [b[n] - b[8 - n] for n in (1, 2, 3)]
    d = [None] + [b[n] + b[8 - n] for n in (1, 2, 3)]
    up, down = b[0] + C2 * c[2], b[0] - C2 * c[2]
    v, w = C1 * c[1] + C3 * c[3], C3 * c[1] - C1 * c[3]
    re1, re7, re3, re5 = up + v, up - v, down + w, down - w
    p, t = C3 * d[1] + C1 * d[3], C2 * d[2] + b[4]
    q, u = C1 * d[1] - C3 * d[3], C2 * d[2] - b[4]
    im1, im7, im3, im5 = -p - t, t - p, -q - u, u - q
    return [(y0, y8), (re1, im1), (re2, im2), (re3, im3), (re4, im4), (re5, im5), (re6, im6), (re7, im7)]


def radix16_back(z):
    (w0, w8), (re1, im1), (re2, im2), (re3, im3), (re4, im4), (re5, im5), (re6, im6), (re7, im7) = z
    plus, minus = w0 + w8, w0 - w8
    ee = [plus + re4, minus - im4, plus - re4, minus + im4]
    m, q = C2 * (re2 - re6), C2 * (im2 + im6)
    eo = [re2 + re6, m - q, im6 - im2, -m - q]
    even = [ee[n] + eo[n] for n in range(4)] + [ee[n] - eo[n] for n in range(4)]
    s17, d17, s35, d35 = re1 + re7, re1 - re7, re3 + re5, re3 - re5
    t17, g17, t35, g35 = im1 + im7, im1 - im7, im3 + im5, im3 - im5
    pc = [None, C1 * d17 + C3 * d35, C2 * (s17 - s35), C3 * d17 - C1 * d35]
    ps = [None, C3 * t17 + C1 * t35, C2 * (g17 + g35), C1 * t17 - C3 * t35]
    odd = [None] * 8
    odd[0] = s17 + s35
    odd[4] = g35 - g17
    for n in (1, 2, 3):
        odd[n] = pc[n] - ps[n]
        odd[8 - n] = -pc[n] - ps[n]
    return [even[n] + odd[n] for n in range(8)] + [even[n] - odd[n] for n in range(8)]


def split(x):
    high = x.astype(BF16)
    return high, (x - high.astype(F32)).astype(BF16)


def dot(a, b):
    return lax.dot_general(a, b, (((1,), (0,)), ((), ())), preferred_element_type=F32)


HALO = 3
SENT = 9
NEAR = 12


def ring(offset, size):
    return min(offset, size - offset)


def forward(source, u, table_hi, table_lo, mix_hi, mix_lo, y, v):
    def forward_rows(block, _):
        parts = []
        for half in range(2):
            x = [source[pl.ds(block * 256 + half * 128 + n1, 8, stride=ROWS), :] for n1 in range(ROWS)]
            parts.append(radix16(x))
        row = pl.multiple_of(block * 16, 16)
        for g in range(GROUPS):
            for part in range(2):
                high, low = split(jnp.concatenate([parts[0][g][part], parts[1][g][part]], axis=0))
                y[g, pl.ds(row, 16), part * 128:(part + 1) * 128] = high
                y[g, pl.ds(row + SHOTS, 16), part * 128:(part + 1) * 128] = low
        return 0

    lax.fori_loop(0, SHOTS // 16, forward_rows, 0)

    for g in range(GROUPS):
        both = dot(y[g], table_hi[g])
        high, low = split(both[:SHOTS] + both[SHOTS:] + dot(y[g, :SHOTS], table_lo[g]))
        c = slice(g * 128, (g + 1) * 128)
        v[0:48, c] = high[:, :128]
        v[48:96, c] = high[:, 128:]
        v[96:144, c] = low[:, :128]
        v[144:192, c] = low[:, 128:]

    for b in range(FREQS // 256):
        c = slice(b * 256, (b + 1) * 256)
        u[:, c] = dot(mix_hi[0], v[:, c]) + dot(mix_lo[0], v[:96, c])


def inverse(u, sweep, q, kept, back_hi, back_lo, mix_hi, mix_lo, y, w, back):
    for b in range(FREQS // 256):
        c = slice(b * 256, (b + 1) * 256)
        keep = kept[sweep * SHOTS:(sweep + 1) * SHOTS, c]
        high, low = split(u[:, c] * jnp.concatenate([keep, keep], axis=0))
        w[:96, c] = high
        w[96:, c] = low

    for b in range(FREQS // 256):
        c = slice(b * 256, (b + 1) * 256)
        high, low = split(dot(mix_hi[1], w[:, c]) + dot(mix_lo[1], w[:96, c]))
        for i in range(2):
            d = slice(i * 128, (i + 1) * 128)
            for part, at in ((high, 0), (low, SHOTS)):
                y[b * 2 + i, at:at + SHOTS, :128] = part[:48, d]
                y[b * 2 + i, at:at + SHOTS, 128:] = part[48:, d]

    for g in range(GROUPS):
        both = dot(y[g], back_hi[g])
        back[g] = both[:SHOTS] + both[SHOTS:] + dot(y[g, :SHOTS], back_lo[g])

    def inverse_rows(block, _):
        row = pl.multiple_of(block * 8, 8)
        z = [
            (back[g, pl.ds(row, 8), 0:128], back[g, pl.ds(row, 8), 128:256])
            for g in range(GROUPS)
        ]
        x = radix16_back(z)
        for n1 in range(ROWS):
            q[pl.ds(row * PITCH + BASE + n1, 8, stride=PITCH), :] = x[n1]
        return 0

    lax.fori_loop(0, SHOTS // 8, inverse_rows, 0)


def fill(sent, record):
    def shots(block, _):
        for i in range(8):
            shot = block * 8 + i
            sent[HALO + shot] = record(pl.ds(pl.multiple_of(shot * PITCH + BASE, 8), ROWS))
        return 0

    lax.fori_loop(0, SHOTS // 8, shots, 0)


def shift_terms(lane, partners, offsets, shot, first, blank):
    terms = []
    for j in range(PARTNERS):
        partner, delay = partners[j, shot], offsets[j, shot]
        trace = jnp.where(partner >= 0, jnp.clip(partner - first, 0, blank - 1), blank)
        rest = delay & 127
        terms.append((trace, BASE - (delay >> 7), rest, lane < 128 - rest))
    return terms


def shifted(load, term):
    trace, start, rest, near = term
    return pltpu.roll(jnp.where(near, load(trace, start), load(trace, start - 1)), rest, 1)


def blend(partners, offsets, q, image, residual=None, sums=0):
    lane = lax.broadcasted_iota(jnp.int32, (ROWS, 128), 1)
    chunk = 8

    def load(trace, start):
        return q[pl.ds(trace * PITCH + start, ROWS), :]

    def shots(block, sums):
        terms = [
            shift_terms(lane, partners, offsets, block * chunk + i, 0, SHOTS) for i in range(chunk)
        ]
        for i in range(chunk):
            shot = block * chunk + i
            g = q[pl.ds(pl.multiple_of(shot * PITCH + BASE, 8), ROWS), :]
            for term in terms[i]:
                g = g + shifted(load, term)
            at = pl.ds(pl.multiple_of(shot * ROWS, ROWS), ROWS)
            image[at, :] = g
            if residual is not None:
                sums = (sums[0] + residual[at, :] * g, sums[1] + g * g)
        return sums

    return lax.fori_loop(0, SHOTS // chunk, shots, sums)


def fold(sums):
    return jnp.concatenate([x[:4] + x[4:8] + x[8:12] + x[12:] for x in sums], axis=0)


def kernel(
    groups,
    partners_h, offsets_h, blended_h, fk_mask_h, order_h, tables_h, mix_hi_h, mix_lo_h,
    out_d, out_r,
    partners, offsets, mix_hi, mix_lo,
    blended, fk_mask, staged, res, q, other, image, image_a, image_b, sent1, sent2, got10, got11, got20, got21,
    left, late, rows_d, rows_r, done_d, done_r,
    y, v, w, back, u0, u1, tables, order, kept, sums_mine, sums_got,
    load_sem, in_send, in_recv, bulk_send, bulk_recv, more_send, more_recv, own_sem, out_sem,
    sum_send, sum_recv,
):
    got1, got2 = (got10, got11), (got20, got21)
    me = lax.axis_index("shot")
    place = lax.axis_index("rcv")
    places = lax.axis_size("rcv")
    core = lax.rem(me, 2)
    mate = (me + 1 - 2 * core, place)
    shot_peers = [(lax.rem(me + k, groups), place) for k in range(1, groups)]
    columns = 8 if places % 8 == 0 else places
    planes = places // columns
    steps = [(i, j) for i in range(planes) for j in range(columns)][1:]
    steps.sort(key=lambda s: -(ring(s[0], planes) + ring(s[1], columns)))
    plane, column = place // columns, lax.rem(place, columns)
    place_peers = [
        (me, lax.rem(plane + i, planes) * columns + lax.rem(column + j, columns)) for i, j in steps
    ]
    peers = shot_peers + place_peers

    barrier = pltpu.get_barrier_semaphore()
    for peer in shot_peers:
        pl.semaphore_signal(barrier, inc=1, device_id=peer, device_id_type=MESH)
    loads = [
        pltpu.make_async_copy(source, target, load_sem.at[i])
        for i, (source, target) in enumerate((
            (blended_h, blended), (mix_hi_h, mix_hi), (mix_lo_h, mix_lo), (fk_mask_h, fk_mask),
            (partners_h, partners), (offsets_h, offsets), (order_h, order), (tables_h, tables),
        ))
    ]
    first_load = loads.pop(0)
    first_load.start()
    for peer in place_peers:
        pl.semaphore_signal(barrier, inc=1, device_id=peer, device_id_type=MESH)

    first_load.wait()
    for load in loads:
        load.start()
    for shot in range(6):
        for half in range(2):
            for n1 in range(ROWS):
                at = half * 8 * 96 + shot * ROWS + n1
                staged[pl.ds(at, 8, stride=96), :] = blended[
                    shot, half * 8:(half + 1) * 8, n1 * 128:(n1 + 1) * 128
                ]

    pl.semaphore_wait(barrier, len(peers))

    mine = pl.ds(pl.multiple_of(me * 96, 8), 96)
    copies = [[], []]
    own = []
    for recv in range(2):
        for k in range(1, groups):
            peer = shot_peers[k - 1]
            copies[recv].append(pltpu.make_async_remote_copy(
                src_ref=staged.at[pl.ds(pl.multiple_of(peer[0] * 192 + recv * 96, 8), 96)],
                dst_ref=res.at[recv, mine],
                send_sem=in_send.at[k - 1, recv],
                recv_sem=in_recv.at[k - 1, recv],
                device_id=peer, device_id_type=MESH,
            ))
            copies[recv][-1].start()
        own.append(pltpu.make_async_copy(
            staged.at[pl.ds(pl.multiple_of(me * 192 + recv * 96, 8), 96)],
            res.at[recv, mine], own_sem.at[recv],
        ))
        own[-1].start()

    q[...] = jnp.zeros_like(q)
    other[...] = jnp.zeros_like(other)
    for sent in (sent1, sent2):
        for recv in range(2):
            blank = jnp.zeros((HALO, ROWS, 128), F32)
            sent[recv, :HALO] = blank
            sent[recv, HALO + SHOTS:] = blank

    def clear(source, _):
        for got in (got1, got2):
            for recv in range(2):
                for trace in range(NEAR):
                    got[recv][source, trace, :BASE, :] = jnp.zeros((BASE, 128), F32)
                    got[recv][source, trace, BASE + ROWS:, :] = jnp.zeros((PITCH - BASE - ROWS, 128), F32)
                got[recv][source, NEAR] = jnp.zeros((PITCH, 128), F32)
        return 0

    lax.fori_loop(0, groups, clear, 0)
    for load in loads:
        load.wait()
    kept[...] = dot(fk_mask[...].astype(F32).astype(BF16), order[...])

    def bulk_start(field, recv, sent, got):
        moves = []
        for k in range(1, groups):
            peer = shot_peers[k - 1]
            there = lax.rem(peer[0], 2)
            moves.append(pltpu.make_async_remote_copy(
                src_ref=sent.at[recv, pl.ds(12 * (peer[0] // 2) + 9 * there, SENT)],
                dst_ref=got[recv].at[me, pl.ds(HALO * there, SENT), pl.ds(BASE, ROWS)],
                send_sem=bulk_send.at[field, k - 1, recv],
                recv_sem=bulk_recv.at[field, k - 1, recv],
                device_id=peer, device_id_type=MESH,
            ))
            moves[-1].start()
        moves.append(pltpu.make_async_copy(
            sent.at[recv, pl.ds(12 * (me // 2) + 9 * core, SENT)],
            got[recv].at[me, pl.ds(HALO * core, SENT), pl.ds(BASE, ROWS)],
            own_sem.at[2 + field * 2 + recv],
        ))
        moves[-1].start()
        return moves

    def more_start(field, recv, got):
        move = pltpu.make_async_remote_copy(
            src_ref=got[recv].at[:, pl.ds(6 - 3 * core, HALO), pl.ds(BASE, ROWS)],
            dst_ref=got[recv].at[:, pl.ds(9 * core, HALO), pl.ds(BASE, ROWS)],
            send_sem=more_send.at[field, recv], recv_sem=more_recv.at[field, recv],
            device_id=mate, device_id_type=MESH,
        )
        move.start()
        return move

    def sum_start(sweep, stage, value):
        sums_mine[sweep, stage] = value
        first = 0 if stage == 0 else len(place_peers)
        moves = []
        for i, peer in enumerate((place_peers, shot_peers)[stage]):
            moves.append(pltpu.make_async_remote_copy(
                src_ref=sums_mine.at[sweep, stage], dst_ref=sums_got.at[sweep, first + i],
                send_sem=sum_send.at[sweep, first + i], recv_sem=sum_recv.at[sweep, first + i],
                device_id=peer, device_id_type=MESH,
            ))
            moves[-1].start()
        return moves

    def sum_end(sweep, stage, value, moves):
        first = 0 if stage == 0 else len(place_peers)
        for i, move in enumerate(moves):
            move.wait_recv()
            value = value + sums_got[sweep, first + i]
        return value

    def ratio(value):
        return jnp.sum(value[:4], keepdims=True) / jnp.sum(value[4:], keepdims=True)

    lane = lax.broadcasted_iota(jnp.int32, (ROWS, 128), 1)
    first_shot = me * 6

    def blend_near(recv, got, put):
        def one_shot(i, _):
            terms = shift_terms(lane, partners, offsets, first_shot + i, first_shot - HALO, NEAR)
            for source in range(groups):
                g = got[recv][source, HALO + i, pl.ds(BASE, ROWS), :]
                for term in terms:
                    g = g + shifted(
                        lambda trace, start: got[recv][source, trace, pl.ds(start, ROWS), :], term
                    )
                put(i, source, g)
            return 0

        lax.fori_loop(0, 6, one_shot, 0)

    ahead = (tables.at[0], tables.at[1], mix_hi, mix_lo, y, v)
    behind = (kept, tables.at[2], tables.at[3], mix_hi, mix_lo, y, w, back)

    zero = jnp.zeros((ROWS, 128), F32)
    sums = (zero, zero)
    bulk1 = []
    for recv in range(2):
        own[recv].wait()
        for copy in copies[recv]:
            copy.wait()
        forward(res.at[recv], u0.at[recv], *ahead)
        inverse(u0.at[recv], 0, q.at[recv], *behind)
        fill(sent1.at[recv], lambda at: q[recv, at, :])
        bulk1.append(bulk_start(0, recv, sent1, got1))
        sums = blend(partners, offsets, q.at[recv], image.at[recv], res.at[recv], sums)
    value = fold(sums)
    stage0 = sum_start(0, 0, value)

    for recv in range(2):
        inverse(u0.at[recv], 1, q.at[recv], *behind)
        blend(partners, offsets, q.at[recv], image_a.at[recv])
    for recv in range(2):
        forward(image.at[recv], u1.at[recv], *ahead)
        inverse(u1.at[recv], 1, other.at[recv], *behind)
    value = sum_end(0, 0, value, stage0)
    stage1 = sum_start(0, 1, value)
    for recv in range(2):
        blend(partners, offsets, other.at[recv], image_b.at[recv])
    value = sum_end(0, 1, value, stage1)
    step1 = ratio(value)

    bulk2 = []
    for recv in range(2):
        fill(sent2.at[recv], lambda at: q[recv, at, :] - step1 * other[recv, at, :])
        bulk2.append(bulk_start(1, recv, sent2, got2))
        if recv == 0:

            def second(block, sums):
                num, den = sums
                for i in range(8):
                    at = pl.ds(pl.multiple_of((block * 8 + i) * ROWS, ROWS), ROWS)
                    for r in range(2):
                        g = image_a[r, at, :] - step1 * image_b[r, at, :]
                        num = num + (res[r, at, :] - step1 * image[r, at, :]) * g
                        den = den + g * g
                return num, den

            value = fold(lax.fori_loop(0, SHOTS // 8, second, (zero, zero)))
            stage2 = sum_start(1, 0, value)

    more1 = []
    for recv in range(2):
        for move in bulk1[recv]:
            move.wait()
        more1.append(more_start(0, recv, got1))
    for recv in range(2):
        more1[recv].wait()

        def put_left(i, source, g):
            old = staged[pl.ds(pl.multiple_of((source * 2 + recv) * 96 + i * ROWS, 8), ROWS), :]
            left[recv, i, source] = old - step1 * g

        blend_near(recv, got1, put_left)

    value = sum_end(1, 0, value, stage2)
    stage3 = sum_start(1, 1, value)

    for move in bulk2[0]:
        move.wait()
    more = more_start(1, 0, got2)
    more.wait()

    def put_late(i, source, g):
        late[i, source] = g

    blend_near(0, got2, put_late)
    for move in bulk2[1]:
        move.wait()
    more = more_start(1, 1, got2)
    value = sum_end(1, 1, value, stage3)
    step2 = ratio(value)

    def rows_of(recv, source):
        return slice((source * 2 + recv) * ROWS, (source * 2 + recv + 1) * ROWS)

    def combine(i, _):
        data = pl.ds(BASE, ROWS)
        for source in range(groups):
            for recv in range(2):
                rows_d[i, rows_of(recv, source), :] = (
                    step1 * got1[recv][source, HALO + i, data, :]
                    + step2 * got2[recv][source, HALO + i, data, :]
                )
            rows_r[i, rows_of(0, source), :] = left[0, i, source] - step2 * late[i, source]
        return 0

    def natural(source, target):
        def one_shot(i, _):
            for half in range(2):
                for n1 in range(ROWS):
                    target[i, half * 8:(half + 1) * 8, n1 * 128:(n1 + 1) * 128] = source[
                        i, pl.ds(half * 128 + n1, 8, stride=ROWS), :
                    ]
            return 0

        lax.fori_loop(0, 6, one_shot, 0)

    lax.fori_loop(0, 6, combine, 0)
    natural(rows_d, done_d)
    write_d = pltpu.make_async_copy(done_d, out_d, out_sem.at[0])
    write_d.start()
    more.wait()

    def put_rest(i, source, g):
        rows_r[i, rows_of(1, source), :] = left[1, i, source] - step2 * g

    blend_near(1, got2, put_rest)
    natural(rows_r, done_r)
    write_r = pltpu.make_async_copy(done_r, out_r, out_sem.at[1])
    write_r.start()
    write_d.wait()
    write_r.wait()

    for move in stage0 + stage1 + stage2 + stage3:
        move.wait_send()


def write_out(d, r, out_d, out_r, held_d, held_r, sem):
    parts = [
        (source.at[i], held.at[i], target.at[i])
        for source, held, target in ((d, held_d, out_d), (r, held_r, out_r))
        for i in range(6)
    ]
    loads = [pltpu.make_async_copy(p[0], p[1], sem.at[0, i]) for i, p in enumerate(parts)]
    stores = [pltpu.make_async_copy(p[1], p[2], sem.at[1, i]) for i, p in enumerate(parts)]
    for load in loads:
        load.start()
    for load, store in zip(loads, stores):
        load.wait()
        store.start()
    for store in stores:
        store.wait()


def solution(mesh):
    groups = mesh.shape["shot"]
    peers = groups - 1 + mesh.shape["rcv"] - 1
    table_hi, table_lo = time_tables()
    tables = np.stack([table_hi, table_lo, table_hi.swapaxes(1, 2), table_lo.swapaxes(1, 2)])
    mix_hi, mix_lo = shot_operands()
    order = mask_order()

    def body(blended, partners, offsets, fk_mask):
        hbm = pl.BlockSpec(memory_space=pltpu.HBM)
        out = jax.ShapeDtypeStruct(blended.shape, F32)
        dma = pltpu.SemaphoreType.DMA
        d, r = pl.pallas_call(
            lambda *refs: kernel(groups, *refs),
            out_shape=(out, out),
            in_specs=[hbm] * 8,
            out_specs=(hbm, hbm),
            scratch_shapes=[
                pltpu.SMEM((PARTNERS, SHOTS), jnp.int32),
                pltpu.SMEM((PARTNERS, SHOTS), jnp.int32),
                pltpu.VMEM(mix_hi.shape, BF16),
                pltpu.VMEM(mix_lo.shape, BF16),
                pltpu.VMEM(blended.shape, F32),
                pltpu.VMEM((ITERATIONS * SHOTS, FREQS), jnp.int32),
                pltpu.VMEM((16 * 96, 128), F32),
                pltpu.VMEM((2, SHOTS * ROWS, 128), F32),
                pltpu.VMEM((2, (SHOTS + 1) * PITCH, 128), F32),
                pltpu.VMEM((2, (SHOTS + 1) * PITCH, 128), F32),
                pltpu.VMEM((2, SHOTS * ROWS, 128), F32),
                pltpu.VMEM((2, SHOTS * ROWS, 128), F32),
                pltpu.VMEM((2, SHOTS * ROWS, 128), F32),
                pltpu.VMEM((2, SHOTS + 2 * HALO, ROWS, 128), F32),
                pltpu.VMEM((2, SHOTS + 2 * HALO, ROWS, 128), F32),
                *[pltpu.VMEM((groups, NEAR + 1, PITCH, 128), F32)] * 4,
                pltpu.VMEM((2, 6, groups, ROWS, 128), F32),
                pltpu.VMEM((6, groups, ROWS, 128), F32),
                pltpu.VMEM((6, 16 * ROWS, 128), F32),
                pltpu.VMEM((6, 16 * ROWS, 128), F32),
                pltpu.VMEM(blended.shape, F32),
                pltpu.VMEM(blended.shape, F32),
                pltpu.VMEM((GROUPS, TRACES, 256), BF16),
                pltpu.VMEM((192, FREQS), BF16),
                pltpu.VMEM((192, FREQS), BF16),
                pltpu.VMEM((GROUPS, SHOTS, 256), F32),
                pltpu.VMEM((2, 96, FREQS), F32),
                pltpu.VMEM((2, 96, FREQS), F32),
                pltpu.VMEM((4, GROUPS, 256, 256), BF16),
                pltpu.VMEM((FREQS, FREQS), BF16),
                pltpu.VMEM((ITERATIONS * SHOTS, FREQS), F32),
                pltpu.VMEM((ITERATIONS, 2, 8, 128), F32),
                pltpu.VMEM((ITERATIONS, peers, 8, 128), F32),
                dma((8,)),
                dma((groups - 1, 2)),
                dma((groups - 1, 2)),
                dma((ITERATIONS, groups - 1, 2)),
                dma((ITERATIONS, groups - 1, 2)),
                dma((ITERATIONS, 2)),
                dma((ITERATIONS, 2)),
                dma((6,)),
                dma((2,)),
                dma((ITERATIONS, peers)),
                dma((ITERATIONS, peers)),
            ],
            compiler_params=pltpu.CompilerParams(
                collective_id=0, has_side_effects=True, vmem_limit_bytes=56 * 2**20
            ),
            name="deblend",
        )(
            partners.T, offsets.T, blended, fk_mask.reshape(ITERATIONS * SHOTS, FREQS),
            jnp.asarray(order), jnp.asarray(tables), jnp.asarray(mix_hi), jnp.asarray(mix_lo),
        )
        return pl.pallas_call(
            write_out,
            out_shape=(out, out),
            in_specs=[hbm, hbm],
            out_specs=(hbm, hbm),
            scratch_shapes=[pltpu.VMEM(blended.shape, F32), pltpu.VMEM(blended.shape, F32), dma((2, 12))],
            compiler_params=pltpu.CompilerParams(vmem_limit_bytes=56 * 2**20),
            name="write_out",
        )(d, r)

    in_specs = (P("shot", "rcv", None), P(), P(), P())
    out_specs = (P("shot", "rcv", None), P("shot", "rcv", None))
    return jax.shard_map(body, mesh=mesh, in_specs=in_specs, out_specs=out_specs, check_vma=False)
```

time: 70.4 us -> 61.2 us (0.87)
  Pallas kernels: 65.4 us -> 60.4 us
  local copies, waits for them, and re-layouts: 4.13 us -> 0 us
    pallas_call x1, Pallas kernels: 65.4 us -> 58.1 us  [body(): pl.pallas_call(lambda *refs: kernel(groups, *refs), out_shape=(out, out),...]
    unnamed x2 -> x0, local copies, waits for them, and re-layouts: 4.13 us -> none
    pallas_call x0 -> x1, Pallas kernels: none -> 2.33 us  [body(): pl.pallas_call(write_out, out_shape=(out, out), in_specs=[hbm, hbm], out_...]
where the time goes in v2:
time: 61.2 us; the launch traced here: 61 us
  Pallas kernels  60.4 us (99%)
  between operations  0.64 us (1%)
    pallas_call x1, Pallas kernels, body(): pl.pallas_call(lambda *refs: kernel(groups, *refs), out_shape=(out, out),...  58.1 us
    pallas_call x1, Pallas kernels, body(): pl.pallas_call(write_out, out_shape=(out, out), in_specs=[hbm, hbm], out_...  2.33 us

profile of v2, /device:TPU:1, one launch (start us, length us, event | category | flops | bytes accessed | tf_op | source)
XLA Modules:
  0.0 61.0 jit_solution(16503942489097151619)
XLA Ops:
  0.6 58.1 %deblend.1 = (f32[6,16,2048]{2,1,0:T(8,128)}, f32[6,16,2048]{2,1,0:T(8,128)}) custom-call(s32[4,48]{1,0:T(4,128)} %bitcast.4, s32[4,48]{1,0:T(4,128)} %bitcast.5, f32[6,16,2048]{2,1,0:T(8,128)} %refs_2_.1, s32[96,1024]{1,0:T(8,128)} %bitcast.3, bf16[1024,1024]{1,0:T(8,128)(2,1)} %constant.8.clone.refs_4_, bf16[4,8,256,256]{3,2,1,0:T(8,128)(2,1)} %constant.9.clone.refs_5_, ...), custom_call_target="tpu_custom_call" | custom-call | tf_op jit(solution)/shard_map/deblend/pallas_call | solution.py:592
  58.7 2.3 %write_out.1 = (f32[6,16,2048]{2,1,0:T(8,128)}, f32[6,16,2048]{2,1,0:T(8,128)}) custom-call(f32[6,16,2048]{2,1,0:T(8,128)} %get-tuple-element.4.d, f32[6,16,2048]{2,1,0:T(8,128)} %get-tuple-element.5.r), custom_call_target="tpu_custom_call" | custom-call | tf_op jit(solution)/shard_map/write_out/pallas_call | solution.py:651

commit v3 on v2

--- a/solution.py
+++ b/solution.py
@@ -137,6 +137,7 @@
 
 
 HALO = 3
+SUM_ORDER = ((0, 1), (1, 0))
 SENT = 9
 NEAR = 12
 
@@ -220,41 +221,47 @@
     lax.fori_loop(0, SHOTS // 8, shots, 0)
 
 
-def shift_terms(lane, partners, offsets, shot, first, blank):
-    terms = []
-    for j in range(PARTNERS):
-        partner, delay = partners[j, shot], offsets[j, shot]
-        trace = jnp.where(partner >= 0, jnp.clip(partner - first, 0, blank - 1), blank)
-        rest = delay & 127
-        terms.append((trace, BASE - (delay >> 7), rest, lane < 128 - rest))
-    return terms
-
-
-def shifted(load, term):
-    trace, start, rest, near = term
-    return pltpu.roll(jnp.where(near, load(trace, start), load(trace, start - 1)), rest, 1)
-
-
-def blend(partners, offsets, q, image, residual=None, sums=0):
+def shift_tables(partners, offsets, traces, rows, rests, count, first_shot, first, blank):
+    def one_shot(i, _):
+        for j in range(PARTNERS):
+            partner, delay = partners[j, first_shot + i], offsets[j, first_shot + i]
+            trace = jnp.where(partner >= 0, jnp.clip(partner - first, 0, blank - 1), blank)
+            if traces is None:
+                rows[j, i] = trace * PITCH + BASE - (delay >> 7)
+            else:
+                traces[j, i] = trace
+                rows[j, i] = BASE - (delay >> 7)
+            rests[j, i] = delay & 127
+        return 0
+
+    lax.fori_loop(0, count, one_shot, 0)
+
+
+def shift_terms(lane, rows, rests, i):
+    return [(rows[j, i], rests[j, i], lane < 128 - rests[j, i]) for j in range(PARTNERS)]
+
+
+def blended_record(own, load, terms):
+    g = own
+    for j, (row, rest, near) in enumerate(terms):
+        g = g + pltpu.roll(jnp.where(near, load(j, row), load(j, row - 1)), rest, 1)
+    return g
+
+
+def blend(tables, fields, residual=None, sums=0, chunk=16):
     lane = lax.broadcasted_iota(jnp.int32, (ROWS, 128), 1)
-    chunk = 8
-
-    def load(trace, start):
-        return q[pl.ds(trace * PITCH + start, ROWS), :]
 
     def shots(block, sums):
-        terms = [
-            shift_terms(lane, partners, offsets, block * chunk + i, 0, SHOTS) for i in range(chunk)
-        ]
+        terms = [shift_terms(lane, *tables, block * chunk + i) for i in range(chunk)]
         for i in range(chunk):
             shot = block * chunk + i
-            g = q[pl.ds(pl.multiple_of(shot * PITCH + BASE, 8), ROWS), :]
-            for term in terms[i]:
-                g = g + shifted(load, term)
             at = pl.ds(pl.multiple_of(shot * ROWS, ROWS), ROWS)
-            image[at, :] = g
-            if residual is not None:
-                sums = (sums[0] + residual[at, :] * g, sums[1] + g * g)
+            for q, image in fields:
+                own = q[pl.ds(pl.multiple_of(shot * PITCH + BASE, 8), ROWS), :]
+                g = blended_record(own, lambda j, row: q[pl.ds(row, ROWS), :], terms[i])
+                image[at, :] = g
+                if residual is not None:
+                    sums = (sums[0] + residual[at, :] * g, sums[1] + g * g)
         return sums
 
     return lax.fori_loop(0, SHOTS // chunk, shots, sums)
@@ -268,11 +275,11 @@
     groups,
     partners_h, offsets_h, blended_h, fk_mask_h, order_h, tables_h, mix_hi_h, mix_lo_h,
     out_d, out_r,
-    partners, offsets, mix_hi, mix_lo,
-    blended, fk_mask, staged, res, q, other, image, image_a, image_b, sent1, sent2, got10, got11, got20, got21,
+    partners, offsets, rows_all, rests_all, traces_near, rows_near, rests_near, mix_hi, mix_lo,
+    blended, fk_mask, staged, res, q, other, image, image_a, image_b, sent1, sent2, raw_a, raw_b, got_a, got_b, got10, got11, got20, got21,
     left, late, rows_d, rows_r, done_d, done_r,
     y, v, w, back, u0, u1, tables, order, kept, sums_mine, sums_got,
-    load_sem, in_send, in_recv, bulk_send, bulk_recv, more_send, more_recv, own_sem, out_sem,
+    load_sem, in_send, in_recv, bulk_send, bulk_recv, raw_send, raw_recv, more_send, more_recv, own_sem, out_sem,
     sum_send, sum_recv,
 ):
     got1, got2 = (got10, got11), (got20, got21)
@@ -360,27 +367,59 @@
     lax.fori_loop(0, groups, clear, 0)
     for load in loads:
         load.wait()
+    first_shot = me * 6
+    shift_tables(partners, offsets, None, rows_all, rests_all, SHOTS, 0, 0, SHOTS)
+    shift_tables(partners, offsets, traces_near, rows_near, rests_near, 6, first_shot, first_shot - HALO, NEAR)
     kept[...] = dot(fk_mask[...].astype(F32).astype(BF16), order[...])
 
-    def bulk_start(field, recv, sent, got):
+    def bulk_start(field, recv, sent, got, part=0):
+        count = (SENT, HALO, SENT - HALO)[part]
+
+        def range_of(device):
+            pair, there = device // 2, lax.rem(device, 2)
+            start = (9 * there, 6 + 3 * there, 12 * there)[part]
+            near = (HALO * there, 6 - 3 * there, 6 * there)[part]
+            return pl.ds(12 * pair + start, count), pl.ds(near, count)
+
+        slot = 2 if part == 1 else recv
         moves = []
         for k in range(1, groups):
             peer = shot_peers[k - 1]
-            there = lax.rem(peer[0], 2)
+            source, target = range_of(peer[0])
             moves.append(pltpu.make_async_remote_copy(
-                src_ref=sent.at[recv, pl.ds(12 * (peer[0] // 2) + 9 * there, SENT)],
-                dst_ref=got[recv].at[me, pl.ds(HALO * there, SENT), pl.ds(BASE, ROWS)],
-                send_sem=bulk_send.at[field, k - 1, recv],
-                recv_sem=bulk_recv.at[field, k - 1, recv],
+                src_ref=sent.at[recv, source],
+                dst_ref=got[recv].at[me, target, pl.ds(BASE, ROWS)],
+                send_sem=bulk_send.at[field, k - 1, slot],
+                recv_sem=bulk_recv.at[field, k - 1, slot],
                 device_id=peer, device_id_type=MESH,
             ))
             moves[-1].start()
+        source, target = range_of(me)
         moves.append(pltpu.make_async_copy(
-            sent.at[recv, pl.ds(12 * (me // 2) + 9 * core, SENT)],
-            got[recv].at[me, pl.ds(HALO * core, SENT), pl.ds(BASE, ROWS)],
-            own_sem.at[2 + field * 2 + recv],
+            sent.at[recv, source],
+            got[recv].at[me, target, pl.ds(BASE, ROWS)],
+            own_sem.at[2 + field * 3 + slot],
         ))
         moves[-1].start()
+        return moves
+
+    def raw_start():
+        moves = []
+        for which, (source, target) in enumerate(((raw_a, got_a), (raw_b, got_b))):
+            for k in range(1, groups):
+                peer = shot_peers[k - 1]
+                start = 12 * (peer[0] // 2) + 6 + 3 * lax.rem(peer[0], 2)
+                moves.append(pltpu.make_async_remote_copy(
+                    src_ref=source.at[pl.ds(start, HALO)], dst_ref=target.at[me],
+                    send_sem=raw_send.at[which, k - 1], recv_sem=raw_recv.at[which, k - 1],
+                    device_id=peer, device_id_type=MESH,
+                ))
+                moves[-1].start()
+            moves.append(pltpu.make_async_copy(
+                source.at[pl.ds(12 * (me // 2) + 6 + 3 * core, HALO)], target.at[me],
+                own_sem.at[8 + which],
+            ))
+            moves[-1].start()
         return moves
 
     def more_start(field, recv, got):
@@ -395,9 +434,10 @@
 
     def sum_start(sweep, stage, value):
         sums_mine[sweep, stage] = value
-        first = 0 if stage == 0 else len(place_peers)
+        group = SUM_ORDER[sweep][stage]
+        first = group * len(place_peers)
         moves = []
-        for i, peer in enumerate((place_peers, shot_peers)[stage]):
+        for i, peer in enumerate((place_peers, shot_peers)[group]):
             moves.append(pltpu.make_async_remote_copy(
                 src_ref=sums_mine.at[sweep, stage], dst_ref=sums_got.at[sweep, first + i],
                 send_sem=sum_send.at[sweep, first + i], recv_sem=sum_recv.at[sweep, first + i],
@@ -407,7 +447,7 @@
         return moves
 
     def sum_end(sweep, stage, value, moves):
-        first = 0 if stage == 0 else len(place_peers)
+        first = SUM_ORDER[sweep][stage] * len(place_peers)
         for i, move in enumerate(moves):
             move.wait_recv()
             value = value + sums_got[sweep, first + i]
@@ -417,26 +457,30 @@
         return jnp.sum(value[:4], keepdims=True) / jnp.sum(value[4:], keepdims=True)
 
     lane = lax.broadcasted_iota(jnp.int32, (ROWS, 128), 1)
-    first_shot = me * 6
-
-    def blend_near(recv, got, put):
-        def one_shot(i, _):
-            terms = shift_terms(lane, partners, offsets, first_shot + i, first_shot - HALO, NEAR)
-            for source in range(groups):
-                g = got[recv][source, HALO + i, pl.ds(BASE, ROWS), :]
-                for term in terms:
-                    g = g + shifted(
-                        lambda trace, start: got[recv][source, trace, pl.ds(start, ROWS), :], term
-                    )
-                put(i, source, g)
+
+    def blend_near(recv, got, put, after=None):
+        def shots(block, _):
+            for i in (block * 2, block * 2 + 1):
+                terms = shift_terms(lane, rows_near, rests_near, i)
+                traces = [traces_near[j, i] for j in range(PARTNERS)]
+                for source in range(groups):
+                    own = got[recv][source, HALO + i, pl.ds(BASE, ROWS), :]
+
+                    def load(j, row):
+                        return got[recv][source, traces[j], pl.ds(row, ROWS), :]
+
+                    put(i, source, blended_record(own, load, terms))
+            if after is not None:
+                after(block)
             return 0
 
-        lax.fori_loop(0, 6, one_shot, 0)
+        lax.fori_loop(0, 3, shots, 0)
 
     ahead = (tables.at[0], tables.at[1], mix_hi, mix_lo, y, v)
     behind = (kept, tables.at[2], tables.at[3], mix_hi, mix_lo, y, w, back)
 
     zero = jnp.zeros((ROWS, 128), F32)
+    shifts = (rows_all, rests_all)
     sums = (zero, zero)
     bulk1 = []
     for recv in range(2):
@@ -446,42 +490,54 @@
         forward(res.at[recv], u0.at[recv], *ahead)
         inverse(u0.at[recv], 0, q.at[recv], *behind)
         fill(sent1.at[recv], lambda at: q[recv, at, :])
-        bulk1.append(bulk_start(0, recv, sent1, got1))
-        sums = blend(partners, offsets, q.at[recv], image.at[recv], res.at[recv], sums)
+        if recv == 0:
+            bulk1.append(bulk_start(0, 0, sent1, got1))
+        sums = blend(shifts, [(q.at[recv], image.at[recv])], res.at[recv], sums)
     value = fold(sums)
     stage0 = sum_start(0, 0, value)
+    bulk1.append(bulk_start(0, 1, sent1, got1))
 
     for recv in range(2):
         inverse(u0.at[recv], 1, q.at[recv], *behind)
-        blend(partners, offsets, q.at[recv], image_a.at[recv])
-    for recv in range(2):
         forward(image.at[recv], u1.at[recv], *ahead)
         inverse(u1.at[recv], 1, other.at[recv], *behind)
+    fill(raw_a, lambda at: q[0, at, :])
+    fill(raw_b, lambda at: other[0, at, :])
+    pairs = ((q, image_a), (other, image_b))
+    blend(shifts, [(f.at[recv], g.at[recv]) for f, g in pairs for recv in range(2)], chunk=4)
     value = sum_end(0, 0, value, stage0)
     stage1 = sum_start(0, 1, value)
-    for recv in range(2):
-        blend(partners, offsets, other.at[recv], image_b.at[recv])
+    raw = raw_start()
     value = sum_end(0, 1, value, stage1)
     step1 = ratio(value)
 
+    def second(block, sums):
+        num, den = sums
+        for i in range(8):
+            at = pl.ds(pl.multiple_of((block * 8 + i) * ROWS, ROWS), ROWS)
+            for r in range(2):
+                g = image_a[r, at, :] - step1 * image_b[r, at, :]
+                num = num + (res[r, at, :] - step1 * image[r, at, :]) * g
+                den = den + g * g
+        return num, den
+
+    value = fold(lax.fori_loop(0, SHOTS // 8, second, (zero, zero)))
+    stage2 = sum_start(1, 0, value)
     bulk2 = []
     for recv in range(2):
         fill(sent2.at[recv], lambda at: q[recv, at, :] - step1 * other[recv, at, :])
-        bulk2.append(bulk_start(1, recv, sent2, got2))
-        if recv == 0:
-
-            def second(block, sums):
-                num, den = sums
-                for i in range(8):
-                    at = pl.ds(pl.multiple_of((block * 8 + i) * ROWS, ROWS), ROWS)
-                    for r in range(2):
-                        g = image_a[r, at, :] - step1 * image_b[r, at, :]
-                        num = num + (res[r, at, :] - step1 * image[r, at, :]) * g
-                        den = den + g * g
-                return num, den
-
-            value = fold(lax.fori_loop(0, SHOTS // 8, second, (zero, zero)))
-            stage2 = sum_start(1, 0, value)
+        if recv == 1:
+            bulk2_mate = bulk_start(1, 1, sent2, got2, 1)
+        bulk2.append(bulk_start(1, recv, sent2, got2, 2))
+
+    for move in raw:
+        move.wait()
+    for source in range(groups):
+        for i in range(HALO):
+            got20[source, 6 - 3 * core + i, BASE:BASE + ROWS, :] = (
+                got_a[source, i] - step1 * got_b[source, i]
+            )
+    more2 = more_start(1, 0, got2)
 
     more1 = []
     for recv in range(2):
@@ -502,14 +558,13 @@
 
     for move in bulk2[0]:
         move.wait()
-    more = more_start(1, 0, got2)
-    more.wait()
+    more2.wait()
 
     def put_late(i, source, g):
         late[i, source] = g
 
     blend_near(0, got2, put_late)
-    for move in bulk2[1]:
+    for move in bulk2_mate:
         move.wait()
     more = more_start(1, 1, got2)
     value = sum_end(1, 1, value, stage3)
@@ -529,32 +584,40 @@
             rows_r[i, rows_of(0, source), :] = left[0, i, source] - step2 * late[i, source]
         return 0
 
-    def natural(source, target):
-        def one_shot(i, _):
-            for half in range(2):
-                for n1 in range(ROWS):
-                    target[i, half * 8:(half + 1) * 8, n1 * 128:(n1 + 1) * 128] = source[
-                        i, pl.ds(half * 128 + n1, 8, stride=ROWS), :
-                    ]
-            return 0
-
-        lax.fori_loop(0, 6, one_shot, 0)
-
+    def natural(source, target, i):
+        for half in range(2):
+            for n1 in range(ROWS):
+                target[i, half * 8:(half + 1) * 8, n1 * 128:(n1 + 1) * 128] = source[
+                    i, pl.ds(half * 128 + n1, 8, stride=ROWS), :
+                ]
+
+    def natural_d(i, _):
+        natural(rows_d, done_d, i)
+        return 0
+
+    def write_r(block):
+        two = pl.ds(block * 2, 2)
+        return pltpu.make_async_copy(done_r.at[two], out_r.at[two], out_sem.at[1 + block])
+
+    def put_rest(i, source, g):
+        rows_r[i, rows_of(1, source), :] = left[1, i, source] - step2 * g
+
+    def finish_r(block):
+        for i in (block * 2, block * 2 + 1):
+            natural(rows_r, done_r, i)
+        write_r(block).start()
+
+    for move in bulk2[1]:
+        move.wait()
     lax.fori_loop(0, 6, combine, 0)
-    natural(rows_d, done_d)
+    more.wait()
+    lax.fori_loop(0, 6, natural_d, 0)
     write_d = pltpu.make_async_copy(done_d, out_d, out_sem.at[0])
     write_d.start()
-    more.wait()
-
-    def put_rest(i, source, g):
-        rows_r[i, rows_of(1, source), :] = left[1, i, source] - step2 * g
-
-    blend_near(1, got2, put_rest)
-    natural(rows_r, done_r)
-    write_r = pltpu.make_async_copy(done_r, out_r, out_sem.at[1])
-    write_r.start()
+    blend_near(1, got2, put_rest, finish_r)
+    for block in range(3):
+        write_r(block).wait()
     write_d.wait()
-    write_r.wait()
 
     for move in stage0 + stage1 + stage2 + stage3:
         move.wait_send()
@@ -595,8 +658,8 @@
             in_specs=[hbm] * 8,
             out_specs=(hbm, hbm),
             scratch_shapes=[
-                pltpu.SMEM((PARTNERS, SHOTS), jnp.int32),
-                pltpu.SMEM((PARTNERS, SHOTS), jnp.int32),
+                *[pltpu.SMEM((PARTNERS, SHOTS), jnp.int32)] * 4,
+                *[pltpu.SMEM((PARTNERS, 6), jnp.int32)] * 3,
                 pltpu.VMEM(mix_hi.shape, BF16),
                 pltpu.VMEM(mix_lo.shape, BF16),
                 pltpu.VMEM(blended.shape, F32),
@@ -610,6 +673,8 @@
                 pltpu.VMEM((2, SHOTS * ROWS, 128), F32),
                 pltpu.VMEM((2, SHOTS + 2 * HALO, ROWS, 128), F32),
                 pltpu.VMEM((2, SHOTS + 2 * HALO, ROWS, 128), F32),
+                *[pltpu.VMEM((SHOTS + 2 * HALO, ROWS, 128), F32)] * 2,
+                *[pltpu.VMEM((groups, HALO, ROWS, 128), F32)] * 2,
                 *[pltpu.VMEM((groups, NEAR + 1, PITCH, 128), F32)] * 4,
                 pltpu.VMEM((2, 6, groups, ROWS, 128), F32),
                 pltpu.VMEM((6, groups, ROWS, 128), F32),
@@ -631,12 +696,14 @@
                 dma((8,)),
                 dma((groups - 1, 2)),
                 dma((groups - 1, 2)),
-                dma((ITERATIONS, groups - 1, 2)),
-                dma((ITERATIONS, groups - 1, 2)),
+                dma((ITERATIONS, groups - 1, 3)),
+                dma((ITERATIONS, groups - 1, 3)),
+                dma((2, groups - 1)),
+                dma((2, groups - 1)),
                 dma((ITERATIONS, 2)),
                 dma((ITERATIONS, 2)),
-                dma((6,)),
-                dma((2,)),
+                dma((10,)),
+                dma((4,)),
                 dma((ITERATIONS, peers)),
                 dma((ITERATIONS, peers)),
             ],

time: 61.2 us -> 59.3 us (0.969)
  Pallas kernels: 60.4 us -> 58.5 us
    pallas_call x1, Pallas kernels: 58.1 us -> 56.2 us  [body(): pl.pallas_call(lambda *refs: kernel(groups, *refs), out_shape=(out, out),...]
where the time goes in v3:
time: 59.3 us; the launch traced here: 59.2 us
  Pallas kernels  58.5 us (99%)
  between operations  0.64 us (1%)
    pallas_call x1, Pallas kernels, body(): pl.pallas_call(lambda *refs: kernel(groups, *refs), out_shape=(out, out),...  56.2 us
    pallas_call x1, Pallas kernels, body(): pl.pallas_call(write_out, out_shape=(out, out), in_specs=[hbm, hbm], out_...  2.33 us

profile of v3, /device:TPU:1, one launch (start us, length us, event | category | flops | bytes accessed | tf_op | source)
XLA Modules:
  0.0 59.2 jit_solution(17770488596436172975)
XLA Ops:
  0.6 56.2 %deblend.1 = (f32[6,16,2048]{2,1,0:T(8,128)}, f32[6,16,2048]{2,1,0:T(8,128)}) custom-call(s32[4,48]{1,0:T(4,128)} %bitcast.4, s32[4,48]{1,0:T(4,128)} %bitcast.5, f32[6,16,2048]{2,1,0:T(8,128)} %refs_2_.1, s32[96,1024]{1,0:T(8,128)} %bitcast.3, bf16[1024,1024]{1,0:T(8,128)(2,1)} %constant.8.clone.refs_4_, bf16[4,8,256,256]{3,2,1,0:T(8,128)(2,1)} %constant.9.clone.refs_5_, ...), custom_call_target="tpu_custom_call" | custom-call | tf_op jit(solution)/shard_map/deblend/pallas_call | solution.py:655
  56.9 2.3 %write_out.1 = (f32[6,16,2048]{2,1,0:T(8,128)}, f32[6,16,2048]{2,1,0:T(8,128)}) custom-call(f32[6,16,2048]{2,1,0:T(8,128)} %get-tuple-element.4.d, f32[6,16,2048]{2,1,0:T(8,128)} %get-tuple-element.5.r), custom_call_target="tpu_custom_call" | custom-call | tf_op jit(solution)/shard_map/write_out/pallas_call | solution.py:718

commit v4 on v3

--- a/solution.py
+++ b/solution.py
@@ -504,10 +504,10 @@
     fill(raw_a, lambda at: q[0, at, :])
     fill(raw_b, lambda at: other[0, at, :])
     pairs = ((q, image_a), (other, image_b))
-    blend(shifts, [(f.at[recv], g.at[recv]) for f, g in pairs for recv in range(2)], chunk=4)
     value = sum_end(0, 0, value, stage0)
     stage1 = sum_start(0, 1, value)
     raw = raw_start()
+    blend(shifts, [(f.at[recv], g.at[recv]) for f, g in pairs for recv in range(2)], chunk=4)
     value = sum_end(0, 1, value, stage1)
     step1 = ratio(value)
 
@@ -552,9 +552,9 @@
             left[recv, i, source] = old - step1 * g
 
         blend_near(recv, got1, put_left)
-
-    value = sum_end(1, 0, value, stage2)
-    stage3 = sum_start(1, 1, value)
+        if recv == 0:
+            value = sum_end(1, 0, value, stage2)
+            stage3 = sum_start(1, 1, value)
 
     for move in bulk2[0]:
         move.wait()
@@ -576,12 +576,11 @@
     def combine(i, _):
         data = pl.ds(BASE, ROWS)
         for source in range(groups):
-            for recv in range(2):
-                rows_d[i, rows_of(recv, source), :] = (
-                    step1 * got1[recv][source, HALO + i, data, :]
-                    + step2 * got2[recv][source, HALO + i, data, :]
-                )
-            rows_r[i, rows_of(0, source), :] = left[0, i, source] - step2 * late[i, source]
+            at = rows_of(0, source)
+            rows_d[i, at, :] = (
+                step1 * got10[source, HALO + i, data, :] + step2 * got20[source, HALO + i, data, :]
+            )
+            rows_r[i, at, :] = left[0, i, source] - step2 * late[i, source]
         return 0
 
     def natural(source, target, i):
@@ -591,33 +590,36 @@
                     i, pl.ds(half * 128 + n1, 8, stride=ROWS), :
                 ]
 
-    def natural_d(i, _):
-        natural(rows_d, done_d, i)
-        return 0
-
-    def write_r(block):
+    def writes(block):
         two = pl.ds(block * 2, 2)
-        return pltpu.make_async_copy(done_r.at[two], out_r.at[two], out_sem.at[1 + block])
+        return (
+            pltpu.make_async_copy(done_d.at[two], out_d.at[two], out_sem.at[block]),
+            pltpu.make_async_copy(done_r.at[two], out_r.at[two], out_sem.at[3 + block]),
+        )
 
     def put_rest(i, source, g):
-        rows_r[i, rows_of(1, source), :] = left[1, i, source] - step2 * g
-
-    def finish_r(block):
+        at = rows_of(1, source)
+        data = pl.ds(BASE, ROWS)
+        rows_r[i, at, :] = left[1, i, source] - step2 * g
+        rows_d[i, at, :] = (
+            step1 * got11[source, HALO + i, data, :] + step2 * got21[source, HALO + i, data, :]
+        )
+
+    def finish_two(block):
         for i in (block * 2, block * 2 + 1):
+            natural(rows_d, done_d, i)
             natural(rows_r, done_r, i)
-        write_r(block).start()
-
+        for write in writes(block):
+            write.start()
+
+    lax.fori_loop(0, 6, combine, 0)
     for move in bulk2[1]:
         move.wait()
-    lax.fori_loop(0, 6, combine, 0)
     more.wait()
-    lax.fori_loop(0, 6, natural_d, 0)
-    write_d = pltpu.make_async_copy(done_d, out_d, out_sem.at[0])
-    write_d.start()
-    blend_near(1, got2, put_rest, finish_r)
+    blend_near(1, got2, put_rest, finish_two)
     for block in range(3):
-        write_r(block).wait()
-    write_d.wait()
+        for write in writes(block):
+            write.wait()
 
     for move in stage0 + stage1 + stage2 + stage3:
         move.wait_send()
@@ -703,7 +705,7 @@
                 dma((ITERATIONS, 2)),
                 dma((ITERATIONS, 2)),
                 dma((10,)),
-                dma((4,)),
+                dma((6,)),
                 dma((ITERATIONS, peers)),
                 dma((ITERATIONS, peers)),
             ],

time: 59.3 us -> 59.2 us (level)
  no operation moved by 1% of the time
where the time goes in v4:
time: 59.2 us; the launch traced here: 59 us
  Pallas kernels  58.4 us (99%)
  between operations  0.64 us (1%)
    pallas_call x1, Pallas kernels, body(): pl.pallas_call(lambda *refs: kernel(groups, *refs), out_shape=(out, out),...  56.1 us
    pallas_call x1, Pallas kernels, body(): pl.pallas_call(write_out, out_shape=(out, out), in_specs=[hbm, hbm], out_...  2.33 us

profile of v4, /device:TPU:1, one launch (start us, length us, event | category | flops | bytes accessed | tf_op | source)
XLA Modules:
  0.0 59.0 jit_solution(1928958829026248968)
XLA Ops:
  0.6 56.1 %deblend.1 = (f32[6,16,2048]{2,1,0:T(8,128)}, f32[6,16,2048]{2,1,0:T(8,128)}) custom-call(s32[4,48]{1,0:T(4,128)} %bitcast.4, s32[4,48]{1,0:T(4,128)} %bitcast.5, f32[6,16,2048]{2,1,0:T(8,128)} %refs_2_.1, s32[96,1024]{1,0:T(8,128)} %bitcast.3, bf16[1024,1024]{1,0:T(8,128)(2,1)} %constant.8.clone.refs_4_, bf16[4,8,256,256]{3,2,1,0:T(8,128)(2,1)} %constant.9.clone.refs_5_, ...), custom_call_target="tpu_custom_call" | custom-call | tf_op jit(solution)/shard_map/deblend/pallas_call | solution.py:657
  56.7 2.3 %write_out.1 = (f32[6,16,2048]{2,1,0:T(8,128)}, f32[6,16,2048]{2,1,0:T(8,128)}) custom-call(f32[6,16,2048]{2,1,0:T(8,128)} %get-tuple-element.4.d, f32[6,16,2048]{2,1,0:T(8,128)} %get-tuple-element.5.r), custom_call_target="tpu_custom_call" | custom-call | tf_op jit(solution)/shard_map/write_out/pallas_call | solution.py:720

commit v5 on v4

--- a/solution.py
+++ b/solution.py
@@ -137,6 +137,7 @@
 
 
 HALO = 3
+FAR_FIRST = (4, 3, 5, 2, 6, 1, 7)
 SUM_ORDER = ((0, 1), (1, 0))
 SENT = 9
 NEAR = 12
@@ -383,7 +384,7 @@
 
         slot = 2 if part == 1 else recv
         moves = []
-        for k in range(1, groups):
+        for k in FAR_FIRST:
             peer = shot_peers[k - 1]
             source, target = range_of(peer[0])
             moves.append(pltpu.make_async_remote_copy(

time: 59.2 us -> 58.4 us (0.986)
  Pallas kernels: 58.4 us -> 57.6 us
    pallas_call x1, Pallas kernels: 56.1 us -> 55.2 us  [body(): pl.pallas_call(lambda *refs: kernel(groups, *refs), out_shape=(out, out),...]
where the time goes in v5:
time: 58.4 us; the launch traced here: 58.2 us
  Pallas kernels  57.6 us (99%)
  between operations  0.64 us (1%)
    pallas_call x1, Pallas kernels, body(): pl.pallas_call(lambda *refs: kernel(groups, *refs), out_shape=(out, out),...  55.2 us
    pallas_call x1, Pallas kernels, body(): pl.pallas_call(write_out, out_shape=(out, out), in_specs=[hbm, hbm], out_...  2.33 us

profile of v5, /device:TPU:1, one launch (start us, length us, event | category | flops | bytes accessed | tf_op | source)
XLA Modules:
  0.0 58.2 jit_solution(17269883802335607759)
XLA Ops:
  0.6 55.2 %deblend.1 = (f32[6,16,2048]{2,1,0:T(8,128)}, f32[6,16,2048]{2,1,0:T(8,128)}) custom-call(s32[4,48]{1,0:T(4,128)} %bitcast.4, s32[4,48]{1,0:T(4,128)} %bitcast.5, f32[6,16,2048]{2,1,0:T(8,128)} %refs_2_.1, s32[96,1024]{1,0:T(8,128)} %bitcast.3, bf16[1024,1024]{1,0:T(8,128)(2,1)} %constant.8.clone.refs_4_, bf16[4,8,256,256]{3,2,1,0:T(8,128)(2,1)} %constant.9.clone.refs_5_, ...), custom_call_target="tpu_custom_call" | custom-call | tf_op jit(solution)/shard_map/deblend/pallas_call | solution.py:658
  55.9 2.3 %write_out.1 = (f32[6,16,2048]{2,1,0:T(8,128)}, f32[6,16,2048]{2,1,0:T(8,128)}) custom-call(f32[6,16,2048]{2,1,0:T(8,128)} %get-tuple-element.4.d, f32[6,16,2048]{2,1,0:T(8,128)} %get-tuple-element.5.r), custom_call_target="tpu_custom_call" | custom-call | tf_op jit(solution)/shard_map/write_out/pallas_call | solution.py:721

commit v6 on v5

--- a/solution.py
+++ b/solution.py
@@ -407,7 +407,7 @@
     def raw_start():
         moves = []
         for which, (source, target) in enumerate(((raw_a, got_a), (raw_b, got_b))):
-            for k in range(1, groups):
+            for k in FAR_FIRST:
                 peer = shot_peers[k - 1]
                 start = 12 * (peer[0] // 2) + 6 + 3 * lax.rem(peer[0], 2)
                 moves.append(pltpu.make_async_remote_copy(

time: 58.4 us -> 58.4 us (level)
  no operation moved by 1% of the time
where the time goes in v6:
time: 58.4 us; the launch traced here: 58.2 us
  Pallas kernels  57.6 us (99%)
  between operations  0.64 us (1%)
    pallas_call x1, Pallas kernels, body(): pl.pallas_call(lambda *refs: kernel(groups, *refs), out_shape=(out, out),...  55.3 us
    pallas_call x1, Pallas kernels, body(): pl.pallas_call(write_out, out_shape=(out, out), in_specs=[hbm, hbm], out_...  2.33 us

profile of v6, /device:TPU:1, one launch (start us, length us, event | category | flops | bytes accessed | tf_op | source)
XLA Modules:
  0.0 58.2 jit_solution(12209785002987129249)
XLA Ops:
  0.6 55.3 %deblend.1 = (f32[6,16,2048]{2,1,0:T(8,128)}, f32[6,16,2048]{2,1,0:T(8,128)}) custom-call(s32[4,48]{1,0:T(4,128)} %bitcast.4, s32[4,48]{1,0:T(4,128)} %bitcast.5, f32[6,16,2048]{2,1,0:T(8,128)} %refs_2_.1, s32[96,1024]{1,0:T(8,128)} %bitcast.3, bf16[1024,1024]{1,0:T(8,128)(2,1)} %constant.8.clone.refs_4_, bf16[4,8,256,256]{3,2,1,0:T(8,128)(2,1)} %constant.9.clone.refs_5_, ...), custom_call_target="tpu_custom_call" | custom-call | tf_op jit(solution)/shard_map/deblend/pallas_call | solution.py:658
  55.9 2.3 %write_out.1 = (f32[6,16,2048]{2,1,0:T(8,128)}, f32[6,16,2048]{2,1,0:T(8,128)}) custom-call(f32[6,16,2048]{2,1,0:T(8,128)} %get-tuple-element.4.d, f32[6,16,2048]{2,1,0:T(8,128)} %get-tuple-element.5.r), custom_call_target="tpu_custom_call" | custom-call | tf_op jit(solution)/shard_map/write_out/pallas_call | solution.py:721
